TPU v7x, 32 devices: a whole 2x2x4 slice. The times are simulated.
32 devices in a mesh: grp: 2 (over x), tm: 8 (over z, y), row: 2 (over core).
Axes of the slice: x: 2, y: 2, z: 4, core: 2. Of those that a mesh axis runs over, the one named last changes fastest.
Arguments:
- frames: bfloat16 [16, 256, 64, 48], P(('grp', 'tm'), None, 'row'), parts along dimension 0, may hold values from 0 to 31, as said below
- clip_start: int32 [16], P('grp'), parts along dimension 0, may hold values 0 or 1
- semantic: int32 [16, 64, 48], P(('grp', 'tm'), 'row'), parts along dimension 0, may hold values from 0 to 18
- instance: int32 [16, 64, 48], P(('grp', 'tm'), 'row'), parts along dimension 0, may hold values from 0 to 63
- aspp_point: bfloat16 [256, 512], replicated, may hold values from -0.25 to 0.25
- aspp_dilated: bfloat16 [3, 9, 256, 512], replicated, may hold values from -0.09375 to 0.09375
- pool_weight: bfloat16 [256, 512], replicated, may hold values from -0.25 to 0.25
- proj_weight: bfloat16 [256, 1280], replicated, may hold values from -0.15625 to 0.15625
- head_weight: bfloat16 [25, 96, 256], replicated, may hold values from -0.078125 to 0.078125
- out_weight: bfloat16 [4, 32], replicated, may hold values from -1 to 1
Outputs:
- predictions: float32 [16, 4, 64, 48], P(('grp', 'tm'), None, 'row'), parts along dimension 0
- losses: float32 [4], P('grp'), parts along dimension 0
There are 2 independent parts, one for each index of `grp`. A program takes and returns all parts, laid end to end along the dimension named above; an argument that names none is the same for every part. Nothing has to cross between parts.
Inputs may be any that keep to these rules, and one draw needn't show every extreme that they name: `frames`: every entry is zero or positive.
All inputs are finite; a program needn't handle non-finite values.
Results may differ from a plain program's by a relative error of at most 0.0075.
Values may be sent and summed in bfloat16 or wider, within the bound.
A program may use at most 128 MiB of HBM per device.

v0:
```python
import jax
import jax.numpy as jnp
from jax import lax
from jax.sharding import PartitionSpec as P

THING_FIRST = 11
INSTANCES = 64


DILATIONS = (6, 12, 18)
aspp_reach = 18
center_sigma = 8.0
offset_weight = 0.01


def padded_2(block, sides, width):
    for axis, dim in sides:
        count = lax.axis_size(axis)
        forward = [(i, i + 1) for i in range(count - 1)]
        backward = [(target, source) for source, target in forward]
        low = lax.ppermute(
            lax.slice_in_dim(block, block.shape[dim] - width, None, axis=dim), axis, forward
        )
        high = lax.ppermute(lax.slice_in_dim(block, 0, width, axis=dim), axis, backward)
        block = jnp.concatenate([low, block, high], axis=dim)
    return block


def shifted(value, axis, steps):
    count = lax.axis_size(axis)
    pairs = [(source, (source + steps) % count) for source in range(count)]
    return lax.ppermute(value, axis, pairs)


def conv_taps(padded, filters, margin, spread, kernel, row_count, col_count):
    running = None
    middle = kernel // 2
    for vertical in range(kernel):
        for lateral in range(kernel):
            row_top = margin + (vertical - middle) * spread
            col_left = margin + (lateral - middle) * spread
            window = padded[:, row_top : row_top + row_count, col_left : col_left + col_count]
            partial_value = jnp.einsum(
                "oc,crw->orw",
                filters[kernel * vertical + lateral],
                window,
                preferred_element_type=jnp.float32,
            )
            running = partial_value if running is None else running + partial_value
    return running


def relu_bf16(values):
    return jnp.maximum(values, 0.0).astype(jnp.bfloat16)


def emit_heads(head_out, out_weight):
    groups = head_out.reshape(3, -1, head_out.shape[1], head_out.shape[2])
    center_map = jnp.einsum(
        "c,crw->rw", out_weight[0], groups[0], preferred_element_type=jnp.float32
    )
    offset_map = jnp.einsum(
        "oc,crw->orw", out_weight[1:3], groups[1], preferred_element_type=jnp.float32
    )
    depth_map = jnp.einsum(
        "c,crw->rw", out_weight[3], groups[2], preferred_element_type=jnp.float32
    )
    return jnp.concatenate([center_map[None], offset_map, depth_map[None]], 0)


def shards(
    frames,
    clip_start,
    semantic,
    instance,
    aspp_point,
    aspp_dilated,
    pool_weight,
    proj_weight,
    head_weight,
    out_weight,
):
    own_band = frames[0]
    channel_count, band_rows, columns = own_band.shape
    frame_count = clip_start.shape[0]
    height = band_rows * lax.axis_size("row")
    time_index = lax.axis_index("tm")
    row_index = lax.axis_index("row")
    ahead = (time_index + 1) % frame_count
    at_end = lax.dynamic_index_in_dim(clip_start, ahead, 0, keepdims=False) == 1
    rim_rows = min(aspp_reach, band_rows)
    own_wide = padded_2(own_band, (("row", 1),), rim_rows)
    later_wide = shifted(own_wide, "tm", -1)
    joined = jnp.concatenate([own_wide, jnp.where(at_end, own_wide, later_wide)], 0)
    extra_rows = aspp_reach - rim_rows
    padded = jnp.pad(joined, ((0, 0), (extra_rows, extra_rows), (aspp_reach, aspp_reach)))
    centre = joined[:, rim_rows : rim_rows + band_rows]
    branches = [
        relu_bf16(jnp.einsum("oc,crw->orw", aspp_point, centre, preferred_element_type=jnp.float32))
    ]
    for branch_index, spread in enumerate(DILATIONS):
        branches.append(
            relu_bf16(
                conv_taps(
                    padded, aspp_dilated[branch_index], aspp_reach, spread, 3, band_rows, columns
                )
            )
        )
    counted = (semantic[0] >= THING_FIRST) & (instance[0] > 0)
    labels = jnp.arange(INSTANCES, dtype=jnp.int32)
    onehot = ((instance[0][None] == labels[:, None, None]) & counted[None]).astype(jnp.float32)
    row_pos = (row_index * band_rows + jnp.arange(band_rows, dtype=jnp.int32)).astype(jnp.float32)[
        :, None
    ] * jnp.ones((1, columns), jnp.float32)
    col_pos = jnp.arange(columns, dtype=jnp.float32)[None, :] * jnp.ones(
        (band_rows, 1), jnp.float32
    )
    local_stats = jnp.stack(
        [
            jnp.sum(onehot, axis=(1, 2)),
            jnp.sum(onehot * row_pos, axis=(1, 2)),
            jnp.sum(onehot * col_pos, axis=(1, 2)),
        ],
        0,
    )
    channel_sums = jnp.sum(centre, axis=(1, 2), dtype=jnp.float32)
    frame_totals, inst_stats = lax.psum((channel_sums, local_stats), "row")
    pooled = (frame_totals / (height * columns)).astype(jnp.bfloat16)
    pool_feature = relu_bf16(jnp.dot(pool_weight, pooled, preferred_element_type=jnp.float32))
    stacked = jnp.concatenate(branches, 0)
    aspp_width = aspp_point.shape[0]
    mixed = jnp.einsum(
        "oc,crw->orw", proj_weight[:, : 4 * aspp_width], stacked, preferred_element_type=jnp.float32
    )
    mixed = (
        mixed
        + jnp.dot(
            proj_weight[:, 4 * aspp_width :], pool_feature, preferred_element_type=jnp.float32
        )[:, None, None]
    )
    projected = relu_bf16(mixed)
    rimmed = padded_2(projected, (("row", 1),), 2)
    head_in = jnp.pad(rimmed, ((0, 0), (0, 0), (2, 2)))
    head_out = relu_bf16(conv_taps(head_in, head_weight, 2, 1, 5, band_rows, columns))
    predictions = emit_heads(head_out, out_weight)
    pixel = jnp.einsum("sk,khw->shw", inst_stats, onehot, precision=lax.Precision.HIGHEST)
    counts = jnp.where(counted, pixel[0], 1.0)
    centre_row = pixel[1] / counts
    centre_col = pixel[2] / counts
    distance = (row_pos - centre_row) * (row_pos - centre_row) + (col_pos - centre_col) * (
        col_pos - centre_col
    )
    heat = jnp.where(counted, jnp.exp(-distance / (2.0 * center_sigma * center_sigma)), 0.0)
    center_err = jnp.sum(jnp.square(predictions[0] - heat))
    offset_err = jnp.sum(
        jnp.where(
            counted,
            jnp.abs(predictions[1] - (centre_row - row_pos))
            + jnp.abs(predictions[2] - (centre_col - col_pos)),
            0.0,
        )
    )
    counted_local = jnp.sum(counted.astype(jnp.float32))
    center_total, offset_total, counted_total = lax.psum(
        (center_err, offset_err, counted_local), ("tm", "row")
    )
    losses = jnp.stack(
        [
            center_total / (frame_count * height * columns),
            offset_weight * offset_total / jnp.maximum(counted_total, 1.0),
        ]
    )
    return (predictions[None], losses)


def solution(mesh):
    placed = (
        P(("grp", "tm"), None, "row", None),
        P("grp"),
        P(("grp", "tm"), "row", None),
        P(("grp", "tm"), "row", None),
        P(),
        P(),
        P(),
        P(),
        P(),
        P(),
    )
    return jax.shard_map(
        shards,
        mesh=mesh,
        in_specs=placed,
        out_specs=(P(("grp", "tm"), None, "row", None), P("grp")),
        check_vma=False,
    )
```

profile of v0, /device:TPU:0, one launch (start us, length us, event | category | flops | bytes accessed | tf_op | source)
XLA Modules:
  0.0 176.8 jit_solution(8292787663885862361)
XLA Ops:
  1.9 2.4 %collective-permute-start = (bf16[256,18,48]{0,2,1:T(8,128)(2,1)S(1)}, bf16[256,18,48]{0,2,1:T(8,128)(2,1)S(1)}, u32[]{:S(2)}, u32[]{:S(2)}) collective-permute-start(bf16[256,18,48]{0,2,1:T(8,128)(2,1)S(1)} %get-tuple-element.19), channel_id=1, source_target_pairs={{0,1},{2,3},{4,5},{6,7},{8,9},{10,11},{12,13},{14,15},{16,17},{18,... | collective-permute-start | bytes 1327112 | tf_op jit(solution)/shard_map/ppermute | solution.py:21
  5.8 2.4 %collective-permute-done.1 = bf16[256,18,48]{0,2,1:T(8,128)(2,1)S(1)} collective-permute-done((bf16[256,18,48]{0,2,1:T(8,128)(2,1)S(1)}, bf16[256,18,48]{0,2,1:T(8,128)(2,1)S(1)}, u32[]{:S(2)}, u32[]{:S(2)}) %collective-permute-start.1) | collective-permute-done | bytes 442400 | tf_op jit(solution)/shard_map/ppermute | solution.py:24
  9.6 5.4 %collective-permute-start.2 = (bf16[256,68,48]{0,2,1:T(8,128)(2,1)}, bf16[256,68,48]{0,2,1:T(8,128)(2,1)}, u32[]{:S(2)}, u32[]{:S(2)}) collective-permute-start(bf16[256,68,48]{0,2,1:T(8,128)(2,1)} %pad_maximum_fusion.1), channel_id=1, source_target_pairs={{0,14},{2,0},{4,2},{6,4},{8,6},{10,8},{12,10},{14,12},{1,15},{3,1}... | collective-permute-start | bytes 5013512 | tf_op jit(solution)/shard_map/ppermute | solution.py:32
  16.9 34.4 %collective-permute-done.2 = bf16[256,68,48]{0,2,1:T(8,128)(2,1)} collective-permute-done((bf16[256,68,48]{0,2,1:T(8,128)(2,1)}, bf16[256,68,48]{0,2,1:T(8,128)(2,1)}, u32[]{:S(2)}, u32[]{:S(2)}) %collective-permute-start.2) | collective-permute-done | bytes 1671200 | tf_op jit(solution)/shard_map/ppermute | solution.py:32
  51.3 1.8 %broadcast_select_fusion = bf16[256,68,48]{0,2,1:T(8,128)(2,1)S(1)} fusion(bf16[256,68,48]{0,2,1:T(8,128)(2,1)} %collective-permute-done.2, pred[]{:T(512)} %bitcast.1, bf16[256,18,48]{0,2,1:T(8,128)(2,1)S(1)} %collective-permute-done.1, bf16[256,32,48]{0,2,1:T(8,128)(2,1)S(1)} %bitcast.366, bf16[256,18,48]{0,2,1:T(8,128)(2,1)S(1)} %collective-permute-done), kind=kLoop, calls=%fused_computation.32 | loop fusion | flops 2506752 | bytes 5013505 | tf_op jit(solution)/shard_map/jit(_where)/select_n | solution.py:94
  53.7 3.6 %fusion.10 = f32[32,48,256]{2,1,0:T(8,128)} fusion(bf16[512,68,48]{0,2,1:T(8,128)(2,1)S(1)} %pad_maximum_fusion, bf16[3,9,256,512]{3,2,1,0:T(8,128)(2,1)} %param.15), kind=kOutput, calls=%fused_computation.34 | convolution fusion | flops 402653184 | bytes 5177344 | tf_op jit(solution)/shard_map/oc,crw->orw/dot_general | solution.py:43
  57.3 1.8 %fusion.11 = f32[32,48,256]{2,1,0:T(8,128)} fusion(bf16[512,68,48]{0,2,1:T(8,128)(2,1)S(1)} %pad_maximum_fusion, bf16[3,9,256,512]{3,2,1,0:T(8,128)(2,1)S(1)} %bitcast.369), kind=kOutput, calls=%fused_computation.35 | convolution fusion | flops 402653184 | bytes 5177344 | tf_op jit(solution)/shard_map/oc,crw->orw/dot_general | solution.py:43
  59.1 1.9 %fusion.12 = f32[32,48,256]{2,1,0:T(8,128)} fusion(bf16[512,68,48]{0,2,1:T(8,128)(2,1)S(1)} %pad_maximum_fusion, bf16[3,9,256,512]{3,2,1,0:T(8,128)(2,1)S(1)} %bitcast.369), kind=kOutput, calls=%fused_computation.36 | convolution fusion | flops 402653184 | bytes 5177344 | tf_op jit(solution)/shard_map/oc,crw->orw/dot_general | solution.py:43
  61.0 1.8 %fusion.124 = f32[32,48,256]{2,1,0:T(8,128)} fusion(bf16[512,68,48]{0,2,1:T(8,128)(2,1)S(1)} %pad_maximum_fusion, bf16[3,9,256,512]{3,2,1,0:T(8,128)(2,1)S(1)} %bitcast.369), kind=kOutput, calls=%fused_computation.169 | convolution fusion | flops 402653184 | bytes 5177344 | tf_op jit(solution)/shard_map/oc,crw->orw/dot_general | solution.py:43
  64.5 1.8 fusion.13
  66.3 1.8 %fusion.132 = f32[32,48,256]{2,1,0:T(8,128)} fusion(bf16[512,68,48]{0,2,1:T(8,128)(2,1)S(1)} %pad_maximum_fusion, bf16[3,9,256,512]{3,2,1,0:T(8,128)(2,1)S(1)} %bitcast.369), kind=kOutput, calls=%fused_computation.177 | convolution fusion | flops 402653184 | bytes 5177344 | tf_op jit(solution)/shard_map/oc,crw->orw/dot_general | solution.py:43
  68.1 1.7 fusion.9
  69.8 1.8 fusion.110
  71.6 1.8 %fusion.114 = f32[32,48,256]{2,1,0:T(8,128)} fusion(bf16[512,68,48]{0,2,1:T(8,128)(2,1)S(1)} %pad_maximum_fusion, bf16[3,9,256,512]{3,2,1,0:T(8,128)(2,1)S(1)} %bitcast.369), kind=kOutput, calls=%fused_computation.161 | convolution fusion | flops 402653184 | bytes 5177344 | tf_op jit(solution)/shard_map/oc,crw->orw/dot_general | solution.py:43
  73.4 1.8 %fusion.118 = f32[32,48,256]{2,1,0:T(8,128)} fusion(bf16[512,68,48]{0,2,1:T(8,128)(2,1)S(1)} %pad_maximum_fusion, bf16[3,9,256,512]{3,2,1,0:T(8,128)(2,1)S(1)} %bitcast.369), kind=kOutput, calls=%fused_computation.165 | convolution fusion | flops 402653184 | bytes 5177344 | tf_op jit(solution)/shard_map/oc,crw->orw/dot_general | solution.py:43
  75.2 1.8 %fusion.15 = f32[32,48,256]{2,1,0:T(8,128)} fusion(bf16[512,68,48]{0,2,1:T(8,128)(2,1)S(1)} %pad_maximum_fusion, bf16[3,9,256,512]{3,2,1,0:T(8,128)(2,1)S(1)} %bitcast.369), kind=kOutput, calls=%fused_computation.39 | convolution fusion | flops 402653184 | bytes 5177344 | tf_op jit(solution)/shard_map/oc,crw->orw/dot_general | solution.py:43
  77.0 1.8 %fusion.16 = f32[32,48,256]{2,1,0:T(8,128)} fusion(bf16[512,68,48]{0,2,1:T(8,128)(2,1)S(1)} %pad_maximum_fusion, bf16[3,9,256,512]{3,2,1,0:T(8,128)(2,1)S(1)} %bitcast.369), kind=kOutput, calls=%fused_computation.40 | convolution fusion | flops 402653184 | bytes 5177344 | tf_op jit(solution)/shard_map/oc,crw->orw/dot_general | solution.py:43
  78.8 1.8 fusion.17
  80.6 1.8 fusion.18
  82.3 1.8 %fusion.19 = f32[32,48,256]{2,1,0:T(8,128)} fusion(bf16[512,68,48]{0,2,1:T(8,128)(2,1)S(1)} %pad_maximum_fusion, bf16[3,9,256,512]{3,2,1,0:T(8,128)(2,1)S(1)} %bitcast.369), kind=kOutput, calls=%fused_computation.43 | convolution fusion | flops 402653184 | bytes 5177344 | tf_op jit(solution)/shard_map/oc,crw->orw/dot_general | solution.py:43
  85.3 1.8 %fusion.21 = f32[32,48,256]{2,1,0:T(8,128)} fusion(bf16[512,68,48]{0,2,1:T(8,128)(2,1)S(1)} %pad_maximum_fusion, bf16[3,9,256,512]{3,2,1,0:T(8,128)(2,1)S(1)} %bitcast.369), kind=kOutput, calls=%fused_computation.45 | convolution fusion | flops 402653184 | bytes 5177344 | tf_op jit(solution)/shard_map/oc,crw->orw/dot_general | solution.py:43
  87.1 1.7 fusion.22
  88.9 1.9 %fusion.23 = f32[32,48,256]{2,1,0:T(8,128)} fusion(bf16[512,68,48]{0,2,1:T(8,128)(2,1)S(1)} %pad_maximum_fusion, bf16[3,9,256,512]{3,2,1,0:T(8,128)(2,1)S(1)} %bitcast.369), kind=kOutput, calls=%fused_computation.47 | convolution fusion | flops 402653184 | bytes 5177344 | tf_op jit(solution)/shard_map/oc,crw->orw/dot_general | solution.py:43
  90.8 1.8 fusion.24
  92.5 2.0 %fusion.25 = f32[32,48,256]{2,1,0:T(8,128)} fusion(bf16[512,68,48]{0,2,1:T(8,128)(2,1)S(1)} %pad_maximum_fusion, bf16[3,9,256,512]{3,2,1,0:T(8,128)(2,1)S(1)} %bitcast.369), kind=kOutput, calls=%fused_computation.49 | convolution fusion | flops 402653184 | bytes 5177344 | tf_op jit(solution)/shard_map/oc,crw->orw/dot_general | solution.py:43
  94.5 1.8 %fusion.96 = f32[32,48,256]{2,1,0:T(8,128)} fusion(bf16[512,68,48]{0,2,1:T(8,128)(2,1)S(1)} %pad_maximum_fusion, bf16[3,9,256,512]{3,2,1,0:T(8,128)(2,1)S(1)} %bitcast.369), kind=kOutput, calls=%fused_computation.145 | convolution fusion | flops 402653184 | bytes 5177344 | tf_op jit(solution)/shard_map/oc,crw->orw/dot_general | solution.py:43
  98.1 2.4 %all-reduce.3 = (f32[512]{0:T(512)S(1)}, f32[3,64]{1,0:T(4,128)S(1)}) all-reduce(f32[512]{0:T(512)S(1)} %convert_reduce_fusion, f32[3,64]{1,0:T(4,128)S(1)} %pad_maximum_fusion.8), channel_id=1, replica_groups=mesh['grp'=2,'tm'=8,'row'=2] {'row'}, use_global_device_ids=true, to_apply=%region_1.2 | all-reduce | flops 704 | bytes 5632 | tf_op jit(solution)/shard_map/psum | solution.py:127
  102.9 6.3 %fusion.78 = bf16[256,32,48]{0,2,1:T(8,128)(2,1)S(1)} fusion(f32[32,48,256]{2,1,0:T(8,128)} %fusion.124, f32[32,48,256]{2,1,0:T(8,128)} %fusion.13, f32[32,48,256]{2,1,0:T(8,128)} %fusion.12, f32[32,48,256]{2,1,0:T(8,128)} %fusion.128, f32[32,48,256]{2,1,0:T(8,128)} %fusion.11, f32[32,48,256]{2,1,0:T(8,128)} %fusion.10, f32[32,48,256]{2,1,0:T(8,128)} %fusion.9, ...), kind=kOutput, calls=%fused_computation.130 | convolution fusion | flops 406585344 | bytes 16973824 | tf_op jit(solution)/shard_map/oc,crw->orw/dot_general | solution.py:43
  112.6 2.1 %fusion.79 = bf16[256,32,48]{0,2,1:T(8,128)(2,1)S(1)} fusion(f32[32,48,256]{2,1,0:T(8,128)S(1)} %copy-done.11, f32[32,48,256]{2,1,0:T(8,128)S(1)} %copy-done.18, f32[32,48,256]{2,1,0:T(8,128)S(1)} %copy-done.17, f32[32,48,256]{2,1,0:T(8,128)S(1)} %copy-done.12, f32[32,48,256]{2,1,0:T(8,128)S(1)} %copy-done.16, f32[32,48,256]{2,1,0:T(8,128)S(1)} %copy-done.15, ...), kind=kOutput, calls=%fused_computation.131 | convolution fusion | flops 406585344 | bytes 16973824 | tf_op jit(solution)/shard_map/oc,crw->orw/dot_general | solution.py:43
  116.4 2.0 %fusion.80 = bf16[256,32,48]{0,2,1:T(8,128)(2,1)S(1)} fusion(f32[32,48,256]{2,1,0:T(8,128)S(1)} %copy-done.10, f32[32,48,256]{2,1,0:T(8,128)S(1)} %copy-done.9, f32[32,48,256]{2,1,0:T(8,128)S(1)} %copy-done.8, f32[32,48,256]{2,1,0:T(8,128)S(1)} %fusion.100, f32[32,48,256]{2,1,0:T(8,128)S(1)} %copy-done.7, f32[32,48,256]{2,1,0:T(8,128)S(1)} %copy-done.6, ...), kind=kOutput, calls=%fused_computation.132 | convolution fusion | flops 406585344 | bytes 16973824 | tf_op jit(solution)/shard_map/oc,crw->orw/dot_general | solution.py:43
  119.7 2.2 %collective-permute-start.3 = (bf16[256,2,48]{0,2,1:T(8,128)(2,1)S(1)}, bf16[256,2,48]{0,2,1:T(8,128)(2,1)S(1)}, u32[]{:S(2)}, u32[]{:S(2)}) collective-permute-start(bf16[256,2,48]{0,2,1:T(8,128)(2,1)S(1)} %get-tuple-element.17), channel_id=1, source_target_pairs={{0,1},{2,3},{4,5},{6,7},{8,9},{10,11},{12,13},{14,15},{16,17},{18,... | collective-permute-start | bytes 147464 | tf_op jit(solution)/shard_map/ppermute | solution.py:21
  138.4 35.9 %all-reduce.2 = (f32[]{:T(128)}, f32[]{:T(128)}, f32[]{:T(128)}) all-reduce(f32[]{:T(128)} %get-tuple-element.5, f32[]{:T(128)} %get-tuple-element.9, f32[]{:T(128)} %get-tuple-element.4), channel_id=1, replica_groups=mesh['grp'=2,'tm'=8,'row'=2] {'tm','row'}, use_global_device_ids=true, to_apply=%region_9.10 | all-reduce | flops 3 | bytes 24 | tf_op jit(solution)/shard_map/psum | solution.py:164
  (120 shorter events, 36.1 us)
Async XLA Ops:
  0.6 96.0 %copy-start = (bf16[256,512]{1,0:T(8,128)(2,1)S(1)}, bf16[256,512]{1,0:T(8,128)(2,1)}, u32[]{:S(2)}) copy-start(bf16[256,512]{1,0:T(8,128)(2,1)} %param.14) | copy-start | bytes 786436
  0.6 7.6 %copy-start.4 = (bf16[1,256,32,48]{1,3,2,0:T(8,128)(2,1)S(1)}, bf16[1,256,32,48]{1,3,2,0:T(8,128)(2,1)}, u32[]{:S(2)}) copy-start(bf16[1,256,32,48]{1,3,2,0:T(8,128)(2,1)} %param.10) | copy-start | bytes 2359300
  1.9 3.9 %collective-permute-start = (bf16[256,18,48]{0,2,1:T(8,128)(2,1)S(1)}, bf16[256,18,48]{0,2,1:T(8,128)(2,1)S(1)}, u32[]{:S(2)}, u32[]{:S(2)}) collective-permute-start(bf16[256,18,48]{0,2,1:T(8,128)(2,1)S(1)} %get-tuple-element.19), channel_id=1, source_target_pairs={{0,1},{2,3},{4,5},{6,7},{8,9},{10,11},{12,13},{14,15},{16,17},{18,... | collective-permute-start | bytes 1327112 | tf_op jit(solution)/shard_map/ppermute | solution.py:21
  4.3 10.6 %copy-start.24 = (s32[8]{0:T(128)S(1)}, s32[8]{0:T(128)}, u32[]{:S(2)}) copy-start(s32[8]{0:T(128)} %param.11) | copy-start | bytes 100
  4.4 11.9 %copy-start.20 = (s32[1,32,48]{2,1,0:T(8,128)S(1)}, s32[1,32,48]{2,1,0:T(8,128)}, u32[]{:S(2)}) copy-start(s32[1,32,48]{2,1,0:T(8,128)} %param.13) | copy-start | bytes 18436
  4.4 11.9 %copy-start.22 = (s32[1,32,48]{2,1,0:T(8,128)S(1)}, s32[1,32,48]{2,1,0:T(8,128)}, u32[]{:S(2)}) copy-start(s32[1,32,48]{2,1,0:T(8,128)} %param.12) | copy-start | bytes 18436
  4.4 3.8 %collective-permute-start.1 = (bf16[256,18,48]{0,2,1:T(8,128)(2,1)S(1)}, bf16[256,18,48]{0,2,1:T(8,128)(2,1)S(1)}, u32[]{:S(2)}, u32[]{:S(2)}) collective-permute-start(bf16[256,18,48]{0,2,1:T(8,128)(2,1)S(1)} %get-tuple-element.20), channel_id=1, source_target_pairs={{1,0},{3,2},{5,4},{7,6},{9,8},{11,10},{13,12},{15,14},{17,16},{19,... | collective-permute-start | bytes 1327112 | tf_op jit(solution)/shard_map/ppermute | solution.py:24
  9.6 41.8 %collective-permute-start.2 = (bf16[256,68,48]{0,2,1:T(8,128)(2,1)}, bf16[256,68,48]{0,2,1:T(8,128)(2,1)}, u32[]{:S(2)}, u32[]{:S(2)}) collective-permute-start(bf16[256,68,48]{0,2,1:T(8,128)(2,1)} %pad_maximum_fusion.1), channel_id=1, source_target_pairs={{0,14},{2,0},{4,2},{6,4},{8,6},{10,8},{12,10},{14,12},{1,15},{3,1}... | collective-permute-start | bytes 5013512 | tf_op jit(solution)/shard_map/ppermute | solution.py:32
  51.3 6.0 %slice-start = ((s8[7077888]{0:T(1024)(128)(4,1)}), s8[4194304]{0:T(1024)(128)(4,1)S(1)}, s32[]{:S(2)}) async-start(s8[7077888]{0:T(1024)(128)(4,1)} %bitcast.368), calls=%async_computation | async-start | bytes 8388608
  53.2 4.1 %slice-start.1 = ((s8[7077888]{0:T(1024)(128)(4,1)}), s8[2883584]{0:T(1024)(128)(4,1)S(1)}, s32[]{:S(2)}) async-start(s8[7077888]{0:T(1024)(128)(4,1)} %bitcast.368), calls=%async_computation.1 | async-start | bytes 5767168
  53.7 42.9 %copy-start.2 = (bf16[512,68,48]{0,2,1:T(8,128)(2,1)}, bf16[512,68,48]{0,2,1:T(8,128)(2,1)S(1)}, u32[]{:S(2)}) copy-start(bf16[512,68,48]{0,2,1:T(8,128)(2,1)S(1)} %pad_maximum_fusion) | copy-start | bytes 10027012
  102.8 6.4 %copy-start.3 = (bf16[512,68,48]{0,2,1:T(8,128)(2,1)S(1)}, bf16[512,68,48]{0,2,1:T(8,128)(2,1)}, u32[]{:S(2)}) copy-start(bf16[512,68,48]{0,2,1:T(8,128)(2,1)} %copy-done.2) | copy-start | bytes 10027012
  102.8 6.6 %copy-start.11 = (f32[32,48,256]{2,1,0:T(8,128)S(1)}, f32[32,48,256]{2,1,0:T(8,128)}, u32[]{:S(2)}) copy-start(f32[32,48,256]{2,1,0:T(8,128)} %fusion.110) | copy-start | bytes 4718596
  102.8 7.1 %copy-start.12 = (f32[32,48,256]{2,1,0:T(8,128)S(1)}, f32[32,48,256]{2,1,0:T(8,128)}, u32[]{:S(2)}) copy-start(f32[32,48,256]{2,1,0:T(8,128)} %fusion.114) | copy-start | bytes 4718596
  102.8 7.6 %copy-start.13 = (f32[32,48,256]{2,1,0:T(8,128)S(1)}, f32[32,48,256]{2,1,0:T(8,128)}, u32[]{:S(2)}) copy-start(f32[32,48,256]{2,1,0:T(8,128)} %fusion.118) | copy-start | bytes 4718596
  102.8 8.0 %copy-start.14 = (f32[32,48,256]{2,1,0:T(8,128)S(1)}, f32[32,48,256]{2,1,0:T(8,128)}, u32[]{:S(2)}) copy-start(f32[32,48,256]{2,1,0:T(8,128)} %fusion.15) | copy-start | bytes 4718596
  102.8 8.4 %copy-start.15 = (f32[32,48,256]{2,1,0:T(8,128)S(1)}, f32[32,48,256]{2,1,0:T(8,128)}, u32[]{:S(2)}) copy-start(f32[32,48,256]{2,1,0:T(8,128)} %fusion.16) | copy-start | bytes 4718596
  102.8 8.8 %copy-start.16 = (f32[32,48,256]{2,1,0:T(8,128)S(1)}, f32[32,48,256]{2,1,0:T(8,128)}, u32[]{:S(2)}) copy-start(f32[32,48,256]{2,1,0:T(8,128)} %fusion.17) | copy-start | bytes 4718596
  102.9 9.3 %copy-start.17 = (f32[32,48,256]{2,1,0:T(8,128)S(1)}, f32[32,48,256]{2,1,0:T(8,128)}, u32[]{:S(2)}) copy-start(f32[32,48,256]{2,1,0:T(8,128)} %fusion.18) | copy-start | bytes 4718596
  102.9 9.7 %copy-start.18 = (f32[32,48,256]{2,1,0:T(8,128)S(1)}, f32[32,48,256]{2,1,0:T(8,128)}, u32[]{:S(2)}) copy-start(f32[32,48,256]{2,1,0:T(8,128)} %fusion.19) | copy-start | bytes 4718596
  112.6 2.1 %copy-start.5 = (f32[32,48,256]{2,1,0:T(8,128)S(1)}, f32[32,48,256]{2,1,0:T(8,128)}, u32[]{:S(2)}) copy-start(f32[32,48,256]{2,1,0:T(8,128)} %fusion.21) | copy-start | bytes 4718596
  112.6 2.1 %copy-start.6 = (f32[32,48,256]{2,1,0:T(8,128)S(1)}, f32[32,48,256]{2,1,0:T(8,128)}, u32[]{:S(2)}) copy-start(f32[32,48,256]{2,1,0:T(8,128)} %fusion.22) | copy-start | bytes 4718596
  112.6 2.4 %copy-start.7 = (f32[32,48,256]{2,1,0:T(8,128)S(1)}, f32[32,48,256]{2,1,0:T(8,128)}, u32[]{:S(2)}) copy-start(f32[32,48,256]{2,1,0:T(8,128)} %fusion.23) | copy-start | bytes 4718596
  112.6 2.9 %copy-start.8 = (f32[32,48,256]{2,1,0:T(8,128)S(1)}, f32[32,48,256]{2,1,0:T(8,128)}, u32[]{:S(2)}) copy-start(f32[32,48,256]{2,1,0:T(8,128)} %fusion.24) | copy-start | bytes 4718596
  112.6 3.4 %copy-start.9 = (f32[32,48,256]{2,1,0:T(8,128)S(1)}, f32[32,48,256]{2,1,0:T(8,128)}, u32[]{:S(2)}) copy-start(f32[32,48,256]{2,1,0:T(8,128)} %fusion.25) | copy-start | bytes 4718596
  112.6 3.8 %copy-start.10 = (f32[32,48,256]{2,1,0:T(8,128)S(1)}, f32[32,48,256]{2,1,0:T(8,128)}, u32[]{:S(2)}) copy-start(f32[32,48,256]{2,1,0:T(8,128)} %fusion.96) | copy-start | bytes 4718596
  116.4 2.0 %copy-start.21 = (bf16[256,1280]{1,0:T(8,128)(2,1)S(1)}, bf16[256,1280]{1,0:T(8,128)(2,1)}, u32[]{:S(2)}) copy-start(bf16[256,1280]{1,0:T(8,128)(2,1)} %param.17) | copy-start | bytes 1966084
  116.4 2.0 %copy-start.25 = (bf16[256,32,48]{0,2,1:T(8,128)(2,1)S(1)}, bf16[256,32,48]{0,2,1:T(8,128)(2,1)}, u32[]{:S(2)}) copy-start(bf16[256,32,48]{0,2,1:T(8,128)(2,1)} %fusion.29) | copy-start | bytes 2359300
  119.7 5.9 %copy-start.19 = (bf16[25,96,256]{2,1,0:T(8,128)(2,1)S(1)}, bf16[25,96,256]{2,1,0:T(8,128)(2,1)}, u32[]{:S(2)}) copy-start(bf16[25,96,256]{2,1,0:T(8,128)(2,1)} %param.18) | copy-start | bytes 3686404
  119.7 5.1 %collective-permute-start.3 = (bf16[256,2,48]{0,2,1:T(8,128)(2,1)S(1)}, bf16[256,2,48]{0,2,1:T(8,128)(2,1)S(1)}, u32[]{:S(2)}, u32[]{:S(2)}) collective-permute-start(bf16[256,2,48]{0,2,1:T(8,128)(2,1)S(1)} %get-tuple-element.17), channel_id=1, source_target_pairs={{0,1},{2,3},{4,5},{6,7},{8,9},{10,11},{12,13},{14,15},{16,17},{18,... | collective-permute-start | bytes 147464 | tf_op jit(solution)/shard_map/ppermute | solution.py:21
  121.9 3.1 %collective-permute-start.4 = (bf16[256,2,48]{0,2,1:T(8,128)(2,1)S(1)}, bf16[256,2,48]{0,2,1:T(8,128)(2,1)S(1)}, u32[]{:S(2)}, u32[]{:S(2)}) collective-permute-start(bf16[256,2,48]{0,2,1:T(8,128)(2,1)S(1)} %get-tuple-element.18), channel_id=1, source_target_pairs={{1,0},{3,2},{5,4},{7,6},{9,8},{11,10},{13,12},{15,14},{17,16},{19,... | collective-permute-start | bytes 147464 | tf_op jit(solution)/shard_map/ppermute | solution.py:24
  134.6 42.2 %copy-start.1 = (bf16[256,512]{1,0:T(8,128)(2,1)S(1)}, bf16[256,512]{1,0:T(8,128)(2,1)}, u32[]{:S(2)}) copy-start(bf16[256,512]{1,0:T(8,128)(2,1)} %param.14) | copy-start | bytes 786436
  (1 other events, 0.7 us)
where the time goes:
time: 177 us
  matrix products  70.3 us (40%)
  blocking collectives  38.3 us (22%)
  waiting for transfers between devices  37 us (21%)
  starting transfers between devices  12.7 us (7%)
  local copies, waits for them, and re-layouts  8.13 us (5%)
  other arithmetic  6.55 us (4%)
  between operations  3.8 us (2%)
    dot_general x52, matrix products, conv_taps(): jnp.einsum('oc,crw->orw', filters[kernel * vertical + lateral], window, p...  62.2 us
    psum x1, blocking collectives, shards(): lax.psum((center_err, offset_err, counted_local), ('tm', 'row'))  35.9 us
    ppermute x1, waiting for transfers between devices, shifted(): return lax.ppermute(value, axis, pairs)  34.4 us
    unnamed x57, local copies, waits for them, and re-layouts  6.12 us
    ppermute x1, starting transfers between devices, shifted(): return lax.ppermute(value, axis, pairs)  5.39 us
    ppermute x2, starting transfers between devices, padded_2(): lax.ppermute(lax.slice_in_dim(block, block.shape[dim] - width, None, axis...  4.59 us
  transfers between devices with their start and end apart: 5, of which 3 were waited for; matrix products, arithmetic and copies ran while one was open for 2% of the time, Pallas kernels for 0%

commit v1 on v0

v1 whole, which is shorter than its diff:
```python
import functools

import jax
import jax.numpy as jnp
import numpy as np
from jax import lax
from jax.experimental import pallas as pl
from jax.experimental.pallas import tpu as pltpu
from jax.sharding import PartitionSpec as P

THING_FIRST = 11
DILATIONS = (6, 12, 18)
REACH = 18
HEAD_REACH = 2
LANES = 128
center_sigma = 8.0
offset_weight = 0.01
MESH = pl.DeviceIdType.MESH


def dot_nt(a, b):
    return lax.dot_general(a, b, (((1,), (1,)), ((), ())), preferred_element_type=jnp.float32)


def dot_nn(a, b):
    return lax.dot_general(a, b, (((1,), (0,)), ((), ())), preferred_element_type=jnp.float32)


def kernel(
    frame_count,
    rows,
    cols,
    tile_rows,
    x_ref,
    flag_ref,
    label_ref,
    place_ref,
    point_hbm,
    dilated_hbm,
    pool_hbm,
    proj_hbm,
    head_hbm,
    out_w_ref,
    pred_ref,
    sums_ref,
    own,
    nxt,
    acc,
    point_w,
    dilated_w,
    pool_w,
    proj_w,
    head_w,
    projected,
    aux,
    small,
    small_in,
    total,
    total_in,
    local_sem,
    send_sem,
    recv_sem,
):
    g = lax.axis_index("grp")
    t = lax.axis_index("tm")
    r = lax.axis_index("row")
    prev = lax.rem(t + frame_count - 1, frame_count)
    later = lax.rem(t + 1, frame_count)
    sister = 1 - r
    cells = rows * cols
    tile = tile_rows * cols
    tiles = rows // tile_rows
    first = REACH * cols
    channels = x_ref.shape[1]
    rim = REACH * cols
    rest = cells - rim

    def local(index, src, dst):
        return pltpu.make_async_copy(src, dst, local_sem.at[index])

    copies = [
        local(0, x_ref, own.at[pl.ds(first, cells)]),
        local(1, dilated_hbm, dilated_w),
        local(2, point_hbm, point_w),
        local(3, pool_hbm, pool_w),
        local(4, proj_hbm, proj_w),
        local(5, head_hbm, head_w.at[:, pl.ds(0, head_hbm.shape[1])]),
    ]
    for copy in copies:
        copy.start()

    barrier = pltpu.get_barrier_semaphore()
    for other in ((g, t, sister), (g, prev, r), (g, later, r)):
        pl.semaphore_signal(barrier, inc=1, device_id=other, device_id_type=MESH)
    pl.semaphore_wait(barrier, 3)

    def remote(index, src, dst, device):
        return pltpu.make_async_remote_copy(
            src_ref=src,
            dst_ref=dst,
            send_sem=send_sem.at[index],
            recv_sem=recv_sem.at[index],
            device_id=device,
            device_id_type=MESH,
        )

    rim_start = pl.multiple_of((rows - REACH) * cols * (1 - r), 16)
    rest_start = pl.multiple_of(rim * r, 16)
    halo_there = pl.multiple_of((REACH + rows) * cols * r, 16)
    halo_zero = pl.multiple_of((REACH + rows) * cols * r, 16)
    rim_mine = pl.multiple_of(first + rim_start, 16)
    rest_mine = pl.multiple_of(first + rest_start, 16)

    own_halo = remote(
        0, x_ref.at[pl.ds(rim_start, rim)], own.at[pl.ds(halo_there, rim)], (g, t, sister)
    )
    next_rim = remote(
        1, x_ref.at[pl.ds(rim_start, rim)], nxt.at[pl.ds(rim_mine, rim)], (g, prev, r)
    )
    next_rest = remote(
        2, x_ref.at[pl.ds(rest_start, rest)], nxt.at[pl.ds(rest_mine, rest)], (g, prev, r)
    )
    next_halo = remote(
        3, nxt.at[pl.ds(rim_mine, rim)], nxt.at[pl.ds(halo_there, rim)], (g, t, sister)
    )
    own_halo.start()
    next_rim.start()
    next_rest.start()

    own[pl.ds(halo_zero, rim), :] = jnp.zeros((rim, channels), own.dtype)
    nxt[pl.ds(halo_zero, rim), :] = jnp.zeros((rim, channels), nxt.dtype)
    edge = HEAD_REACH * cols
    edge_zero = pl.multiple_of((HEAD_REACH + rows) * cols * r, 16)
    projected[pl.ds(edge_zero, edge), :] = jnp.zeros((edge, channels), projected.dtype)
    head_taps, head_width = head_hbm.shape[0], head_hbm.shape[1]
    head_w[:, pl.ds(head_width, LANES - head_width), :] = jnp.zeros(
        (head_taps, LANES - head_width, channels), head_w.dtype
    )

    label = label_ref[...]
    ids = lax.broadcasted_iota(jnp.int32, (LANES, cells), 0)
    onehot = jnp.where((ids == label) & (label > 0), 1.0, 0.0).astype(jnp.bfloat16)
    band_top = (r * rows).astype(jnp.float32)
    kind = lax.broadcasted_iota(jnp.int32, (8, cells), 0)
    place = place_ref[...] + jnp.where(kind == 1, band_top, 0.0)
    stats = dot_nt(place.astype(jnp.bfloat16), onehot)
    copies[0].wait()
    ones = jnp.ones((8, cells), jnp.bfloat16)
    channel_sums = dot_nn(ones, own[pl.ds(first, cells), :])
    small[:, :LANES] = stats
    small[:, LANES:] = channel_sums
    swap = remote(4, small, small_in, (g, t, sister))
    swap.start()
    swap.wait()
    total[...] = small[:, LANES:] + small_in[:, LANES:]
    frame_total = remote(5, total, total_in, (g, prev, r))
    frame_total.start()
    full_stats = small[:, :LANES] + small_in[:, :LANES]
    means = full_stats / jnp.maximum(full_stats[0:1], 1.0)
    high = means.astype(jnp.bfloat16)
    left = means - high.astype(jnp.float32)
    middle = left.astype(jnp.bfloat16)
    low = (left - middle.astype(jnp.float32)).astype(jnp.bfloat16)
    centre = dot_nn(high, onehot) + (dot_nn(middle, onehot) + dot_nn(low, onehot))
    aim = centre - place
    square = aim * aim
    counted = label > 0
    heat = jnp.where(
        counted,
        jnp.exp(-(square[1:2] + square[2:3]) / (2.0 * center_sigma * center_sigma)),
        0.0,
    )
    aux[...] = jnp.where(kind == 0, heat, aim)

    for copy in copies[1:]:
        copy.wait()

    col = lax.broadcasted_iota(jnp.int32, (tile_rows, cols, LANES), 1).reshape(tile, LANES)

    def widened(mask, width):
        return jnp.concatenate([mask] * (width // LANES), axis=1)

    def moved(value, step):
        width = value.shape[1]
        turned = pltpu.roll(value, (-step) % tile, 0)
        if step > 0:
            keep = col < cols - step
        else:
            keep = col >= -step
        return jnp.where(widened(keep, width), turned, 0.0)

    def branch_sums(source, base, part):
        lanes = pl.ds(part * channels, channels)
        centre_rows = source[pl.ds(pl.multiple_of(base, 16), tile), :]
        results = [dot_nt(centre_rows, point_w[:, lanes])]
        for b, spread in enumerate(DILATIONS):
            window = jnp.concatenate(
                [
                    source[pl.ds(pl.multiple_of(base - spread * cols, 16), tile), :],
                    centre_rows,
                    source[pl.ds(pl.multiple_of(base + spread * cols, 16), tile), :],
                ],
                axis=1,
            )
            value = None
            for j in (0, -1, 1):
                taps = jnp.concatenate(
                    [dilated_w[9 * b + 3 * i + j + 1, :, lanes] for i in range(3)], axis=1
                )
                piece = dot_nt(window, taps)
                if j != 0:
                    piece = moved(piece, j * spread)
                value = piece if value is None else value + piece
            results.append(value)
        return results

    own_halo.wait()

    def own_tile(k, carry):
        base = first + k * tile
        for b, value in enumerate(branch_sums(own, base, 0)):
            acc[b, pl.ds(pl.multiple_of(k * tile, 16), tile), :] = value
        return carry

    lax.fori_loop(0, tiles, own_tile, 0)

    next_rim.wait_recv()
    next_halo.start()

    frame_total.wait()
    clip_end = flag_ref[0, 0] == 1
    later_total = jnp.where(clip_end, total[...], total_in[...])
    pooled = jnp.concatenate(
        [
            (total[...] / (2.0 * cells)).astype(jnp.bfloat16),
            (later_total / (2.0 * cells)).astype(jnp.bfloat16),
        ],
        axis=1,
    )
    feature = jnp.maximum(dot_nt(pooled, pool_w[...]), 0.0).astype(jnp.bfloat16)
    width = point_w.shape[0]
    bias = dot_nt(feature, proj_w[:, pl.ds(4 * width, width)])[0:1]

    next_rim.wait_send()
    next_rest.wait()
    next_halo.wait()

    @pl.loop(0, (rows + 2 * REACH) // 4)
    def _(k):
        spot = pl.ds(pl.multiple_of(k * 4 * cols, 16), 4 * cols)
        nxt[spot, :] = jnp.where(clip_end, own[spot, :], nxt[spot, :])

    edge_src = pl.multiple_of((HEAD_REACH + (rows - HEAD_REACH) * (1 - r)) * cols, 16)
    edge_dst = pl.multiple_of((HEAD_REACH + rows) * cols * r, 16)
    edge_copy = remote(
        6,
        projected.at[pl.ds(edge_src, edge)],
        projected.at[pl.ds(edge_dst, edge)],
        (g, t, sister),
    )

    def next_tile(s, carry):
        k = r * s + (1 - r) * (tiles - 1 - s)
        base = first + k * tile
        spot = pl.ds(pl.multiple_of(k * tile, 16), tile)
        mixed = bias
        for b, value in enumerate(branch_sums(nxt, base, 1)):
            branch = jnp.maximum(value + acc[b, spot, :], 0.0).astype(jnp.bfloat16)
            mixed = mixed + dot_nt(branch, proj_w[:, pl.ds(b * width, width)])
        projected[pl.ds(pl.multiple_of((HEAD_REACH * cols) + k * tile, 16), tile), :] = jnp.maximum(
            mixed, 0.0
        ).astype(jnp.bfloat16)

        @pl.when(s == 0)
        def _():
            edge_copy.start()

        return carry

    lax.fori_loop(0, tiles, next_tile, 0)
    edge_copy.wait()

    size = 2 * HEAD_REACH + 1

    def head_tile(k, carry):
        base = HEAD_REACH * cols + k * tile
        window = jnp.concatenate(
            [
                projected[pl.ds(pl.multiple_of(base + (i - HEAD_REACH) * cols, 16), tile), :]
                for i in range(size)
            ],
            axis=1,
        )
        value = None
        for j in range(size):
            taps = jnp.concatenate([head_w[size * i + j] for i in range(size)], axis=1)
            piece = dot_nt(window, taps)
            if j != HEAD_REACH:
                piece = moved(piece, j - HEAD_REACH)
            value = piece if value is None else value + piece
        head = jnp.maximum(value, 0.0).astype(jnp.bfloat16)
        pred_ref[:, pl.ds(pl.multiple_of(k * tile, LANES), tile)] = dot_nt(out_w_ref[...], head)
        return carry

    lax.fori_loop(0, tiles, head_tile, 0)

    gap = pred_ref[...] - aux[...]
    center_err = jnp.sum(jnp.where(kind == 0, gap * gap, 0.0))
    offset_err = jnp.sum(jnp.where(((kind == 1) | (kind == 2)) & counted, jnp.abs(gap), 0.0))
    number = jnp.sum(jnp.where(counted, 1.0, 0.0))
    lane = lax.broadcasted_iota(jnp.int32, (8, LANES), 1)
    sums_ref[...] = jnp.where(
        lane == 0,
        center_err,
        jnp.where(lane == 1, offset_err, jnp.where(lane == 2, number, 0.0)),
    )


def shards(
    frames,
    clip_start,
    semantic,
    instance,
    aspp_point,
    aspp_dilated,
    pool_weight,
    proj_weight,
    head_weight,
    out_weight,
):
    _, channels, rows, cols = frames.shape
    cells = rows * cols
    frame_count = clip_start.shape[0]
    height = rows * lax.axis_size("row")
    width = aspp_point.shape[0]
    tile_rows = 8
    x = frames[0].reshape(channels, cells).T
    ahead = (lax.axis_index("tm") + 1) % frame_count
    flag = lax.dynamic_slice_in_dim(clip_start, ahead, 1).reshape(1, 1)
    label = jnp.where(semantic[0] >= THING_FIRST, instance[0], 0).reshape(1, cells)
    place = np.zeros((8, cells), np.float32)
    place[0] = 1.0
    place[1] = np.arange(cells) // cols
    place[2] = np.arange(cells) % cols
    part = out_weight.shape[1]
    group = np.minimum((np.arange(8) + 1) // 2, 2)
    out_w = jnp.where(
        np.arange(LANES)[None] // part == group[:, None],
        jnp.tile(jnp.pad(out_weight, ((0, 4), (0, 0))), (1, LANES // part)),
        0,
    )
    vmem = pl.BlockSpec(memory_space=pltpu.VMEM)
    anywhere = pl.BlockSpec(memory_space=pl.ANY)
    taps = aspp_dilated.shape[0] * aspp_dilated.shape[1]
    head_taps = head_weight.shape[0]
    tall = cells + 2 * REACH * cols
    bf16, f32 = jnp.bfloat16, jnp.float32
    pred, sums = pl.pallas_call(
        functools.partial(kernel, frame_count, rows, cols, tile_rows),
        out_shape=(
            jax.ShapeDtypeStruct((8, cells), f32),
            jax.ShapeDtypeStruct((8, LANES), f32),
        ),
        in_specs=[
            anywhere,
            pl.BlockSpec(memory_space=pltpu.SMEM),
            vmem,
            vmem,
            anywhere,
            anywhere,
            anywhere,
            anywhere,
            anywhere,
            vmem,
        ],
        out_specs=(vmem, vmem),
        scratch_shapes=[
            pltpu.VMEM((tall, channels), bf16),
            pltpu.VMEM((tall, channels), bf16),
            pltpu.VMEM((4, cells, width), f32),
            pltpu.VMEM(aspp_point.shape, bf16),
            pltpu.VMEM((taps,) + aspp_dilated.shape[2:], bf16),
            pltpu.VMEM(pool_weight.shape, bf16),
            pltpu.VMEM(proj_weight.shape, bf16),
            pltpu.VMEM((head_taps, LANES, width), bf16),
            pltpu.VMEM((cells + 2 * HEAD_REACH * cols, width), bf16),
            pltpu.VMEM((8, cells), f32),
            pltpu.VMEM((8, LANES + channels), f32),
            pltpu.VMEM((8, LANES + channels), f32),
            pltpu.VMEM((8, channels), f32),
            pltpu.VMEM((8, channels), f32),
            pltpu.SemaphoreType.DMA((6,)),
            pltpu.SemaphoreType.DMA((7,)),
            pltpu.SemaphoreType.DMA((7,)),
        ],
        compiler_params=pltpu.CompilerParams(
            collective_id=0, has_side_effects=True, vmem_limit_bytes=56 * 1024 * 1024
        ),
    )(
        x,
        flag,
        label,
        jnp.asarray(place),
        aspp_point,
        aspp_dilated.reshape((taps,) + aspp_dilated.shape[2:]),
        pool_weight,
        proj_weight,
        head_weight,
        out_w,
    )
    predictions = pred[:4].reshape(1, 4, rows, cols)
    totals = lax.psum(sums[0, :3], ("tm", "row"))
    losses = jnp.stack(
        [
            totals[0] / (frame_count * height * cols),
            offset_weight * totals[1] / jnp.maximum(totals[2], 1.0),
        ]
    )
    return (predictions, losses)


def solution(mesh):
    placed = (
        P(("grp", "tm"), None, "row", None),
        P("grp"),
        P(("grp", "tm"), "row", None),
        P(("grp", "tm"), "row", None),
        P(),
        P(),
        P(),
        P(),
        P(),
        P(),
    )
    return jax.shard_map(
        shards,
        mesh=mesh,
        in_specs=placed,
        out_specs=(P(("grp", "tm"), None, "row", None), P("grp")),
        check_vma=False,
    )
```

time: 177 us -> 85 us (0.48)
  matrix products: 70.3 us -> 0 us
  Pallas kernels: 0 us -> 40.5 us
  waiting for transfers between devices: 37 us -> 0 us
  starting transfers between devices: 12.7 us -> 0 us
  blocking collectives: 38.3 us -> 33.2 us
  other arithmetic: 6.55 us -> 2.02 us
  local copies, waits for them, and re-layouts: 8.13 us -> 6.13 us
    dot_general x60 -> x0, matrix products: 70.3 us -> none  [the longest x52 62.2 us: conv_taps(): jnp.einsum('oc,crw->orw', filters[kernel * vertical + lateral], window, p...]
    pallas_call x0 -> x1, Pallas kernels: none -> 40.5 us  [shards(): pl.pallas_call(functools.partial(kernel, frame_count, rows, cols, tile_ro...]
    ppermute x5 -> x0, waiting for transfers between devices: 37 us -> none  [the longest x1 34.4 us: shifted(): return lax.ppermute(value, axis, pairs)]
    ppermute x5 -> x0, starting transfers between devices: 12.7 us -> none  [the longest x1 5.39 us: shifted(): return lax.ppermute(value, axis, pairs)]
    unnamed x57 -> x0, local copies, waits for them, and re-layouts: 6.12 us -> none
    psum x2 -> x1, blocking collectives: 38.3 us -> 33.2 us  [shards(): totals = lax.psum(sums[0, :3], ('tm', 'row'))]
    concatenate x3 -> x0, other arithmetic: 2.35 us -> none  [the longest x2 1.88 us: padded_2(): block = jnp.concatenate([low, block, high], axis=dim)]
  transfers between devices with their start and end apart: 5 -> 0, of which waited for: 3 -> 0; matrix products, arithmetic and copies ran while one was open for 2% -> 0% of each run, Pallas kernels for 0% -> 0%
where the time goes in v1:
time: 85 us; the launch traced here: 84.6 us
  Pallas kernels  40.5 us (48%)
  blocking collectives  33.2 us (39%)
  local copies, waits for them, and re-layouts  6.13 us (7%)
  between operations  2.69 us (3%)
  other arithmetic  2.02 us (2%)
    pallas_call x1, Pallas kernels, shards(): pl.pallas_call(functools.partial(kernel, frame_count, rows, cols, tile_ro...  40.5 us
    psum x1, blocking collectives, shards(): totals = lax.psum(sums[0, :3], ('tm', 'row'))  33.2 us

profile of v1, /device:TPU:0, one launch (start us, length us, event | category | flops | bytes accessed | tf_op | source)
XLA Modules:
  0.0 84.6 jit_solution(11681182800465338930)
XLA Ops:
  0.6 1.2 %dynamic_slice.3 = s32[1]{0:T(128)} dynamic-slice(s32[8]{0:T(128)} %param.13, s32[]{:T(128)S(6)} %select_n.29), dynamic_slice_sizes={1} | dynamic-slice | bytes 12 | tf_op jit(solution)/shard_map/dynamic_slice | solution.py:339
  1.9 0.7 pad.4
  2.6 0.7 broadcast_select_fusion
  3.3 0.7 reshape.56.out_w_ref
  3.9 0.7 compare_select_fusion
  4.7 0.7 select_n.31.label_ref
  5.3 40.5 %shard_map.131 = (f32[8,1536]{1,0:T(8,128)}, f32[8,128]{1,0:T(8,128)}) custom-call(bf16[1536,256]{1,0:T(8,128)(2,1)} %bitcast.8, s32[1,1]{1,0:T(1,128)} %bitcast.2.flag_ref, s32[1,1536]{1,0:T(1,128)} %select_n.31.label_ref, f32[8,1536]{1,0:T(8,128)} %constant.41.clone.place_ref, bf16[256,512]{1,0:T(8,128)(2,1)} %point_hbm.1, bf16[27,256,512]{2,1,0:T(8,128)(2,1)} %bitcast.7, ...), custom_call_target="tpu_custom_call" | custom-call | tf_op jit(solution)/shard_map/pallas_call | solution.py:358
  45.9 0.8 slice.15
  46.7 0.7 slice_bitcast_fusion
  47.4 33.2 %psum.7 = f32[3]{0:T(128)S(1)} all-reduce(f32[3]{0:T(128)S(1)} %slice_bitcast_fusion), channel_id=1, replica_groups=mesh['grp'=2,'tm'=8,'row'=2] {'tm','row'}, use_global_device_ids=true, to_apply=%region_0.1 | all-reduce | flops 3 | bytes 24 | tf_op jit(solution)/shard_map/psum | solution.py:412
  80.6 0.7 fusion
  83.3 0.6 pad_maximum_fusion
  83.8 0.7 reshape.53

commit v2 on v1

--- a/solution.py
+++ b/solution.py
@@ -2,7 +2,6 @@
 
 import jax
 import jax.numpy as jnp
-import numpy as np
 from jax import lax
 from jax.experimental import pallas as pl
 from jax.experimental.pallas import tpu as pltpu
@@ -32,9 +31,9 @@
     cols,
     tile_rows,
     x_ref,
-    flag_ref,
-    label_ref,
-    place_ref,
+    clip_ref,
+    semantic_ref,
+    instance_ref,
     point_hbm,
     dilated_hbm,
     pool_hbm,
@@ -42,7 +41,7 @@
     head_hbm,
     out_w_ref,
     pred_ref,
-    sums_ref,
+    losses_ref,
     own,
     nxt,
     acc,
@@ -52,14 +51,22 @@
     proj_w,
     head_w,
     projected,
-    aux,
+    heat_map,
+    aim_map,
+    out_full,
     small,
     small_in,
     total,
     total_in,
+    err,
+    err_in,
+    err_pair,
+    err_all,
     local_sem,
     send_sem,
     recv_sem,
+    all_send_sem,
+    all_recv_sem,
 ):
     g = lax.axis_index("grp")
     t = lax.axis_index("tm")
@@ -90,9 +97,10 @@
         copy.start()
 
     barrier = pltpu.get_barrier_semaphore()
-    for other in ((g, t, sister), (g, prev, r), (g, later, r)):
+    others = [lax.rem(t + step, frame_count) for step in range(1, frame_count)]
+    for other in [(g, t, sister)] + [(g, frame, r) for frame in others]:
         pl.semaphore_signal(barrier, inc=1, device_id=other, device_id_type=MESH)
-    pl.semaphore_wait(barrier, 3)
+    pl.semaphore_wait(barrier, frame_count)
 
     def remote(index, src, dst, device):
         return pltpu.make_async_remote_copy(
@@ -137,13 +145,24 @@
         (head_taps, LANES - head_width, channels), head_w.dtype
     )
 
-    label = label_ref[...]
-    ids = lax.broadcasted_iota(jnp.int32, (LANES, cells), 0)
-    onehot = jnp.where((ids == label) & (label > 0), 1.0, 0.0).astype(jnp.bfloat16)
-    band_top = (r * rows).astype(jnp.float32)
-    kind = lax.broadcasted_iota(jnp.int32, (8, cells), 0)
-    place = place_ref[...] + jnp.where(kind == 1, band_top, 0.0)
-    stats = dot_nt(place.astype(jnp.bfloat16), onehot)
+    shape = (8, cols)
+    ids = lax.broadcasted_iota(jnp.int32, (LANES, cols), 0)
+    kind = lax.broadcasted_iota(jnp.int32, shape, 0)
+    across = lax.broadcasted_iota(jnp.int32, shape, 1).astype(jnp.float32)
+    band_top = r * rows
+    label = jnp.where(semantic_ref[0] >= THING_FIRST, instance_ref[0], 0)
+
+    def onehot_row(y):
+        row = label[y : y + 1]
+        return jnp.where((ids == row) & (row > 0), 1.0, 0.0).astype(jnp.bfloat16)
+
+    def place_row(y):
+        down = (band_top + y).astype(jnp.float32)
+        return jnp.where(kind == 0, 1.0, jnp.where(kind == 1, down, across))
+
+    stats = jnp.zeros((8, LANES), jnp.float32)
+    for y in range(rows):
+        stats = stats + dot_nt(place_row(y).astype(jnp.bfloat16), onehot_row(y))
     copies[0].wait()
     ones = jnp.ones((8, cells), jnp.bfloat16)
     channel_sums = dot_nn(ones, own[pl.ds(first, cells), :])
@@ -161,16 +180,29 @@
     left = means - high.astype(jnp.float32)
     middle = left.astype(jnp.bfloat16)
     low = (left - middle.astype(jnp.float32)).astype(jnp.bfloat16)
-    centre = dot_nn(high, onehot) + (dot_nn(middle, onehot) + dot_nn(low, onehot))
-    aim = centre - place
-    square = aim * aim
+    parts = jnp.concatenate([high, middle, low], axis=0)
+    for top in range(0, rows, 8):
+        aims = []
+        for y in range(top, top + 8):
+            centre = dot_nn(parts, onehot_row(y))
+            aims.append(centre[0:8] + (centre[8:16] + centre[16:24]) - place_row(y))
+        for axis in range(2):
+            aim_map[axis, pl.ds(top, 8), :] = jnp.concatenate(
+                [aim[axis + 1 : axis + 2] for aim in aims], axis=0
+            )
     counted = label > 0
-    heat = jnp.where(
-        counted,
-        jnp.exp(-(square[1:2] + square[2:3]) / (2.0 * center_sigma * center_sigma)),
-        0.0,
-    )
-    aux[...] = jnp.where(kind == 0, heat, aim)
+    square = aim_map[0] * aim_map[0] + aim_map[1] * aim_map[1]
+    heat_map[...] = jnp.where(
+        counted, jnp.exp(-square / (2.0 * center_sigma * center_sigma)), 0.0
+    )
+
+    part = out_w_ref.shape[1]
+    out_full[...] = jnp.zeros(out_full.shape, jnp.float32)
+    plain = out_w_ref[...].astype(jnp.float32)
+    wide = jnp.concatenate([plain] * (LANES // part), axis=1)
+    channel = lax.broadcasted_iota(jnp.int32, wide.shape, 0)
+    group = lax.broadcasted_iota(jnp.int32, wide.shape, 1) // part
+    out_full[pl.ds(0, 4), :] = jnp.where(group == (channel + 1) // 2, wide, 0.0)
 
     for copy in copies[1:]:
         copy.wait()
@@ -228,7 +260,7 @@
     next_halo.start()
 
     frame_total.wait()
-    clip_end = flag_ref[0, 0] == 1
+    clip_end = clip_ref[later] == 1
     later_total = jnp.where(clip_end, total[...], total_in[...])
     pooled = jnp.concatenate(
         [
@@ -299,21 +331,55 @@
                 piece = moved(piece, j - HEAD_REACH)
             value = piece if value is None else value + piece
         head = jnp.maximum(value, 0.0).astype(jnp.bfloat16)
-        pred_ref[:, pl.ds(pl.multiple_of(k * tile, LANES), tile)] = dot_nt(out_w_ref[...], head)
+        weights = out_full[...].astype(jnp.bfloat16)
+        maps = [
+            dot_nt(weights, head[y * cols : (y + 1) * cols]) for y in range(tile_rows)
+        ]
+        for c in range(4):
+            pred_ref[0, c, pl.ds(pl.multiple_of(k * tile_rows, 8), tile_rows), :] = (
+                jnp.concatenate([value[c : c + 1] for value in maps], axis=0)
+            )
         return carry
 
     lax.fori_loop(0, tiles, head_tile, 0)
 
-    gap = pred_ref[...] - aux[...]
-    center_err = jnp.sum(jnp.where(kind == 0, gap * gap, 0.0))
-    offset_err = jnp.sum(jnp.where(((kind == 1) | (kind == 2)) & counted, jnp.abs(gap), 0.0))
-    number = jnp.sum(jnp.where(counted, 1.0, 0.0))
-    lane = lax.broadcasted_iota(jnp.int32, (8, LANES), 1)
-    sums_ref[...] = jnp.where(
-        lane == 0,
-        center_err,
-        jnp.where(lane == 1, offset_err, jnp.where(lane == 2, number, 0.0)),
-    )
+    gap = pred_ref[0, 0] - heat_map[...]
+    offset_gap = jnp.abs(pred_ref[0, 1] - aim_map[0]) + jnp.abs(pred_ref[0, 2] - aim_map[1])
+    err[...] = jnp.zeros(err.shape, jnp.float32)
+    err[0:1, pl.ds(0, cols)] = jnp.sum(gap * gap, axis=0, keepdims=True)
+    err[1:2, pl.ds(0, cols)] = jnp.sum(
+        jnp.where(counted, offset_gap, 0.0), axis=0, keepdims=True
+    )
+    err[2:3, pl.ds(0, cols)] = jnp.sum(jnp.where(counted, 1.0, 0.0), axis=0, keepdims=True)
+    pair = remote(7, err, err_in, (g, t, sister))
+    pair.start()
+    pair.wait()
+    err_pair[...] = err[...] + err_in[...]
+    err_all[t] = err_pair[...]
+
+    def spread_copy(step, slot):
+        return pltpu.make_async_remote_copy(
+            src_ref=err_pair,
+            dst_ref=err_all.at[slot],
+            send_sem=all_send_sem.at[step],
+            recv_sem=all_recv_sem.at[slot],
+            device_id=(g, others[step], r),
+            device_id_type=MESH,
+        )
+
+    for step in range(frame_count - 1):
+        spread_copy(step, t).start()
+    for step in range(frame_count - 1):
+        spread_copy(step, t).wait_send()
+        spread_copy(step, others[step]).wait_recv()
+    summed = err_all[0]
+    for frame in range(1, frame_count):
+        summed = summed + err_all[frame]
+    sums = jnp.sum(summed, axis=1, keepdims=True)
+    center_loss = sums[0:1] / (frame_count * 2 * cells)
+    offset_loss = offset_weight * sums[1:2] / jnp.maximum(sums[2:3], 1.0)
+    losses_ref[0] = center_loss[0, 0]
+    losses_ref[1] = offset_loss[0, 0]
 
 
 def shards(
@@ -331,35 +397,20 @@
     _, channels, rows, cols = frames.shape
     cells = rows * cols
     frame_count = clip_start.shape[0]
-    height = rows * lax.axis_size("row")
     width = aspp_point.shape[0]
     tile_rows = 8
     x = frames[0].reshape(channels, cells).T
-    ahead = (lax.axis_index("tm") + 1) % frame_count
-    flag = lax.dynamic_slice_in_dim(clip_start, ahead, 1).reshape(1, 1)
-    label = jnp.where(semantic[0] >= THING_FIRST, instance[0], 0).reshape(1, cells)
-    place = np.zeros((8, cells), np.float32)
-    place[0] = 1.0
-    place[1] = np.arange(cells) // cols
-    place[2] = np.arange(cells) % cols
-    part = out_weight.shape[1]
-    group = np.minimum((np.arange(8) + 1) // 2, 2)
-    out_w = jnp.where(
-        np.arange(LANES)[None] // part == group[:, None],
-        jnp.tile(jnp.pad(out_weight, ((0, 4), (0, 0))), (1, LANES // part)),
-        0,
-    )
     vmem = pl.BlockSpec(memory_space=pltpu.VMEM)
     anywhere = pl.BlockSpec(memory_space=pl.ANY)
     taps = aspp_dilated.shape[0] * aspp_dilated.shape[1]
     head_taps = head_weight.shape[0]
     tall = cells + 2 * REACH * cols
     bf16, f32 = jnp.bfloat16, jnp.float32
-    pred, sums = pl.pallas_call(
+    return pl.pallas_call(
         functools.partial(kernel, frame_count, rows, cols, tile_rows),
         out_shape=(
-            jax.ShapeDtypeStruct((8, cells), f32),
-            jax.ShapeDtypeStruct((8, LANES), f32),
+            jax.ShapeDtypeStruct((1, 4, rows, cols), f32),
+            jax.ShapeDtypeStruct((2,), f32),
         ),
         in_specs=[
             anywhere,
@@ -373,7 +424,7 @@
             anywhere,
             vmem,
         ],
-        out_specs=(vmem, vmem),
+        out_specs=(vmem, pl.BlockSpec(memory_space=pltpu.SMEM)),
         scratch_shapes=[
             pltpu.VMEM((tall, channels), bf16),
             pltpu.VMEM((tall, channels), bf16),
@@ -384,39 +435,38 @@
             pltpu.VMEM(proj_weight.shape, bf16),
             pltpu.VMEM((head_taps, LANES, width), bf16),
             pltpu.VMEM((cells + 2 * HEAD_REACH * cols, width), bf16),
-            pltpu.VMEM((8, cells), f32),
+            pltpu.VMEM((rows, cols), f32),
+            pltpu.VMEM((2, rows, cols), f32),
+            pltpu.VMEM((8, LANES), f32),
             pltpu.VMEM((8, LANES + channels), f32),
             pltpu.VMEM((8, LANES + channels), f32),
             pltpu.VMEM((8, channels), f32),
             pltpu.VMEM((8, channels), f32),
+            pltpu.VMEM((8, LANES), f32),
+            pltpu.VMEM((8, LANES), f32),
+            pltpu.VMEM((8, LANES), f32),
+            pltpu.VMEM((frame_count, 8, LANES), f32),
             pltpu.SemaphoreType.DMA((6,)),
-            pltpu.SemaphoreType.DMA((7,)),
-            pltpu.SemaphoreType.DMA((7,)),
+            pltpu.SemaphoreType.DMA((8,)),
+            pltpu.SemaphoreType.DMA((8,)),
+            pltpu.SemaphoreType.DMA((frame_count - 1,)),
+            pltpu.SemaphoreType.DMA((frame_count,)),
         ],
         compiler_params=pltpu.CompilerParams(
             collective_id=0, has_side_effects=True, vmem_limit_bytes=56 * 1024 * 1024
         ),
     )(
         x,
-        flag,
-        label,
-        jnp.asarray(place),
+        clip_start,
+        semantic,
+        instance,
         aspp_point,
         aspp_dilated.reshape((taps,) + aspp_dilated.shape[2:]),
         pool_weight,
         proj_weight,
         head_weight,
-        out_w,
-    )
-    predictions = pred[:4].reshape(1, 4, rows, cols)
-    totals = lax.psum(sums[0, :3], ("tm", "row"))
-    losses = jnp.stack(
-        [
-            totals[0] / (frame_count * height * cols),
-            offset_weight * totals[1] / jnp.maximum(totals[2], 1.0),
-        ]
-    )
-    return (predictions, losses)
+        out_weight,
+    )
 
 
 def solution(mesh):

time: 85 us -> 51.1 us (0.60)
  blocking collectives: 33.2 us -> 0 us
  Pallas kernels: 40.5 us -> 47.6 us
  local copies, waits for them, and re-layouts: 6.13 us -> 2.59 us
  between operations: 2.69 us -> 0.64 us
  other arithmetic: 2.02 us -> 0 us
    psum x1 -> x0, blocking collectives: 33.2 us -> none  [shards(): totals = lax.psum(sums[0, :3], ('tm', 'row'))]
    pallas_call x1, Pallas kernels: 40.5 us -> 47.6 us  [shards(): pl.pallas_call(functools.partial(kernel, frame_count, rows, cols, tile_ro...]
    unnamed x0 -> x2, local copies, waits for them, and re-layouts: none -> 2.59 us
    slice x2 -> x0, local copies, waits for them, and re-layouts: 1.47 us -> none  [the longest x1 0.8 us: shards(): predictions = pred[:4].reshape(1, 4, rows, cols)]
    select_n x2 -> x0, other arithmetic: 1.44 us -> none  [the longest x1 0.74 us: shards(): jnp.where(semantic[0] >= THING_FIRST, instance[0], 0).reshape(1, cells)]
    select_n x2 -> x0, local copies, waits for them, and re-layouts: 1.33 us -> none  [the longest x1 0.68 us: shards(): jnp.where(semantic[0] >= THING_FIRST, instance[0], 0).reshape(1, cells)]
    dynamic_slice x1 -> x0, local copies, waits for them, and re-layouts: 1.24 us -> none  [shards(): flag = lax.dynamic_slice_in_dim(clip_start, ahead, 1).reshape(1, 1)]
where the time goes in v2:
time: 51.1 us; the launch traced here: 50.8 us
  Pallas kernels  47.6 us (93%)
  local copies, waits for them, and re-layouts  2.59 us (5%)
  between operations  0.64 us (1%)
    pallas_call x1, Pallas kernels, shards(): pl.pallas_call(functools.partial(kernel, frame_count, rows, cols, tile_ro...  47.6 us
    unnamed x2, local copies, waits for them, and re-layouts  2.59 us

profile of v2, /device:TPU:0, one launch (start us, length us, event | category | flops | bytes accessed | tf_op | source)
XLA Modules:
  0.0 50.8 jit_solution(14321655408568052027)
XLA Ops:
  0.6 47.6 %shard_map.113 = (f32[1,4,32,48]{3,2,1,0:T(8,128)}, f32[2]{0:T(128)}) custom-call(bf16[1536,256]{1,0:T(8,128)(2,1)} %bitcast.5, s32[8]{0:T(128)} %clip_ref.1, s32[1,32,48]{2,1,0:T(8,128)} %semantic_ref.1, s32[1,32,48]{2,1,0:T(8,128)} %instance_ref.1, bf16[256,512]{1,0:T(8,128)(2,1)} %point_hbm.1, bf16[27,256,512]{2,1,0:T(8,128)(2,1)} %bitcast.4, ...), custom_call_target="tpu_custom_call" | custom-call | tf_op jit(solution)/shard_map/pallas_call | solution.py:409
  48.2 1.5 %copy.14 = f32[1,4,32,48]{3,2,1,0:T(8,128)} copy(f32[1,4,32,48]{3,2,1,0:T(8,128)} %get-tuple-element.4) | data formatting | bytes 49152
  49.7 1.1 %copy.15 = f32[2]{0:T(128)} copy(f32[2]{0:T(128)} %get-tuple-element.5) | data formatting | bytes 16

commit v3 on v2

--- a/solution.py
+++ b/solution.py
@@ -2,6 +2,7 @@
 
 import jax
 import jax.numpy as jnp
+import numpy as np
 from jax import lax
 from jax.experimental import pallas as pl
 from jax.experimental.pallas import tpu as pltpu
@@ -34,6 +35,7 @@
     clip_ref,
     semantic_ref,
     instance_ref,
+    place_ref,
     point_hbm,
     dilated_hbm,
     pool_hbm,
@@ -145,24 +147,14 @@
         (head_taps, LANES - head_width, channels), head_w.dtype
     )
 
-    shape = (8, cols)
-    ids = lax.broadcasted_iota(jnp.int32, (LANES, cols), 0)
-    kind = lax.broadcasted_iota(jnp.int32, shape, 0)
-    across = lax.broadcasted_iota(jnp.int32, shape, 1).astype(jnp.float32)
-    band_top = r * rows
     label = jnp.where(semantic_ref[0] >= THING_FIRST, instance_ref[0], 0)
-
-    def onehot_row(y):
-        row = label[y : y + 1]
-        return jnp.where((ids == row) & (row > 0), 1.0, 0.0).astype(jnp.bfloat16)
-
-    def place_row(y):
-        down = (band_top + y).astype(jnp.float32)
-        return jnp.where(kind == 0, 1.0, jnp.where(kind == 1, down, across))
-
-    stats = jnp.zeros((8, LANES), jnp.float32)
-    for y in range(rows):
-        stats = stats + dot_nt(place_row(y).astype(jnp.bfloat16), onehot_row(y))
+    flat = jnp.concatenate([label[y : y + 1] for y in range(rows)], axis=1)
+    ids = lax.broadcasted_iota(jnp.int32, (LANES, cells), 0)
+    onehot = jnp.where((ids == flat) & (flat > 0), 1.0, 0.0).astype(jnp.bfloat16)
+    band_top = (r * rows).astype(jnp.float32)
+    kind = lax.broadcasted_iota(jnp.int32, (8, cells), 0)
+    place = place_ref[...] + jnp.where(kind == 1, band_top, 0.0)
+    stats = dot_nt(place.astype(jnp.bfloat16), onehot)
     copies[0].wait()
     ones = jnp.ones((8, cells), jnp.bfloat16)
     channel_sums = dot_nn(ones, own[pl.ds(first, cells), :])
@@ -181,15 +173,12 @@
     middle = left.astype(jnp.bfloat16)
     low = (left - middle.astype(jnp.float32)).astype(jnp.bfloat16)
     parts = jnp.concatenate([high, middle, low], axis=0)
-    for top in range(0, rows, 8):
-        aims = []
-        for y in range(top, top + 8):
-            centre = dot_nn(parts, onehot_row(y))
-            aims.append(centre[0:8] + (centre[8:16] + centre[16:24]) - place_row(y))
-        for axis in range(2):
-            aim_map[axis, pl.ds(top, 8), :] = jnp.concatenate(
-                [aim[axis + 1 : axis + 2] for aim in aims], axis=0
-            )
+    centre = dot_nn(parts, onehot)
+    aim = centre[0:8] + (centre[8:16] + centre[16:24]) - place
+    for axis in range(2):
+        aim_map[axis] = jnp.concatenate(
+            [aim[axis + 1 : axis + 2, y * cols : (y + 1) * cols] for y in range(rows)], axis=0
+        )
     counted = label > 0
     square = aim_map[0] * aim_map[0] + aim_map[1] * aim_map[1]
     heat_map[...] = jnp.where(
@@ -398,7 +387,11 @@
     cells = rows * cols
     frame_count = clip_start.shape[0]
     width = aspp_point.shape[0]
-    tile_rows = 8
+    tile_rows = 16
+    place = np.zeros((8, cells), np.float32)
+    place[0] = 1.0
+    place[1] = np.arange(cells) // cols
+    place[2] = np.arange(cells) % cols
     x = frames[0].reshape(channels, cells).T
     vmem = pl.BlockSpec(memory_space=pltpu.VMEM)
     anywhere = pl.BlockSpec(memory_space=pl.ANY)
@@ -415,6 +408,7 @@
         in_specs=[
             anywhere,
             pl.BlockSpec(memory_space=pltpu.SMEM),
+            vmem,
             vmem,
             vmem,
             anywhere,
@@ -460,6 +454,7 @@
         clip_start,
         semantic,
         instance,
+        jnp.asarray(place),
         aspp_point,
         aspp_dilated.reshape((taps,) + aspp_dilated.shape[2:]),
         pool_weight,

time: 51.1 us -> 49.8 us (0.975)
  Pallas kernels: 47.6 us -> 46.4 us
    pallas_call x1, Pallas kernels: 47.6 us -> 46.4 us  [shards(): pl.pallas_call(functools.partial(kernel, frame_count, rows, cols, tile_ro...]
where the time goes in v3:
time: 49.8 us; the launch traced here: 49.6 us
  Pallas kernels  46.4 us (93%)
  local copies, waits for them, and re-layouts  2.59 us (5%)
  between operations  0.64 us (1%)
    pallas_call x1, Pallas kernels, shards(): pl.pallas_call(functools.partial(kernel, frame_count, rows, cols, tile_ro...  46.4 us
    unnamed x2, local copies, waits for them, and re-layouts  2.59 us

profile of v3, /device:TPU:0, one launch (start us, length us, event | category | flops | bytes accessed | tf_op | source)
XLA Modules:
  0.0 49.6 jit_solution(11622866918985109821)
XLA Ops:
  0.6 46.4 %shard_map.122 = (f32[1,4,32,48]{3,2,1,0:T(8,128)}, f32[2]{0:T(128)}) custom-call(bf16[1536,256]{1,0:T(8,128)(2,1)} %bitcast.5, s32[8]{0:T(128)} %clip_ref.1, s32[1,32,48]{2,1,0:T(8,128)} %semantic_ref.1, s32[1,32,48]{2,1,0:T(8,128)} %instance_ref.1, f32[8,1536]{1,0:T(8,128)} %constant.2.clone.place_ref, bf16[256,512]{1,0:T(8,128)(2,1)} %point_hbm.1, ...), custom_call_target="tpu_custom_call" | custom-call | tf_op jit(solution)/shard_map/pallas_call | solution.py:402
  47.0 1.5 %copy.15 = f32[1,4,32,48]{3,2,1,0:T(8,128)} copy(f32[1,4,32,48]{3,2,1,0:T(8,128)} %get-tuple-element.4) | data formatting | bytes 49152
  48.5 1.1 %copy.16 = f32[2]{0:T(128)} copy(f32[2]{0:T(128)} %get-tuple-element.5) | data formatting | bytes 16

commit v4 on v3

--- a/solution.py
+++ b/solution.py
@@ -11,6 +11,7 @@
 THING_FIRST = 11
 DILATIONS = (6, 12, 18)
 REACH = 18
+EARLY = 20
 HEAD_REACH = 2
 LANES = 128
 center_sigma = 8.0
@@ -61,8 +62,6 @@
     total,
     total_in,
     err,
-    err_in,
-    err_pair,
     err_all,
     local_sem,
     send_sem,
@@ -82,7 +81,8 @@
     first = REACH * cols
     channels = x_ref.shape[1]
     rim = REACH * cols
-    rest = cells - rim
+    early = EARLY * cols
+    rest = cells - early
 
     def local(index, src, dst):
         return pltpu.make_async_copy(src, dst, local_sem.at[index])
@@ -99,10 +99,14 @@
         copy.start()
 
     barrier = pltpu.get_barrier_semaphore()
-    others = [lax.rem(t + step, frame_count) for step in range(1, frame_count)]
-    for other in [(g, t, sister)] + [(g, frame, r) for frame in others]:
-        pl.semaphore_signal(barrier, inc=1, device_id=other, device_id_type=MESH)
-    pl.semaphore_wait(barrier, frame_count)
+    bands = 2 * frame_count
+    mine = 2 * t + r
+    slots = [lax.rem(mine + step, bands) for step in range(1, bands)]
+    for slot in slots:
+        pl.semaphore_signal(
+            barrier, inc=1, device_id=(g, slot // 2, slot % 2), device_id_type=MESH
+        )
+    pl.semaphore_wait(barrier, bands - 1)
 
     def remote(index, src, dst, device):
         return pltpu.make_async_remote_copy(
@@ -115,7 +119,9 @@
         )
 
     rim_start = pl.multiple_of((rows - REACH) * cols * (1 - r), 16)
-    rest_start = pl.multiple_of(rim * r, 16)
+    early_start = pl.multiple_of((cells - early) * (1 - r), 16)
+    rest_start = pl.multiple_of(early * r, 16)
+    early_mine = pl.multiple_of(first + early_start, 16)
     halo_there = pl.multiple_of((REACH + rows) * cols * r, 16)
     halo_zero = pl.multiple_of((REACH + rows) * cols * r, 16)
     rim_mine = pl.multiple_of(first + rim_start, 16)
@@ -124,8 +130,8 @@
     own_halo = remote(
         0, x_ref.at[pl.ds(rim_start, rim)], own.at[pl.ds(halo_there, rim)], (g, t, sister)
     )
-    next_rim = remote(
-        1, x_ref.at[pl.ds(rim_start, rim)], nxt.at[pl.ds(rim_mine, rim)], (g, prev, r)
+    next_early = remote(
+        1, x_ref.at[pl.ds(early_start, early)], nxt.at[pl.ds(early_mine, early)], (g, prev, r)
     )
     next_rest = remote(
         2, x_ref.at[pl.ds(rest_start, rest)], nxt.at[pl.ds(rest_mine, rest)], (g, prev, r)
@@ -134,7 +140,7 @@
         3, nxt.at[pl.ds(rim_mine, rim)], nxt.at[pl.ds(halo_there, rim)], (g, t, sister)
     )
     own_halo.start()
-    next_rim.start()
+    next_early.start()
     next_rest.start()
 
     own[pl.ds(halo_zero, rim), :] = jnp.zeros((rim, channels), own.dtype)
@@ -210,23 +216,33 @@
             keep = col >= -step
         return jnp.where(widened(keep, width), turned, 0.0)
 
-    def branch_sums(source, base, part):
+    inner = 1 - 2 * r
+    outer_half = r * (tiles - 1)
+    inner_half = (1 - r) * (tiles - 1)
+
+    def branch_sums(source, half, part, plan, with_point):
         lanes = pl.ds(part * channels, channels)
-        centre_rows = source[pl.ds(pl.multiple_of(base, 16), tile), :]
-        results = [dot_nt(centre_rows, point_w[:, lanes])]
+        base = first + half * tile
+        results = [None]
+        if with_point:
+            rows_here = source[pl.ds(pl.multiple_of(base, 16), tile), :]
+            results = [dot_nt(rows_here, point_w[:, lanes])]
         for b, spread in enumerate(DILATIONS):
+            if not plan[b]:
+                results.append(None)
+                continue
             window = jnp.concatenate(
                 [
-                    source[pl.ds(pl.multiple_of(base - spread * cols, 16), tile), :],
-                    centre_rows,
-                    source[pl.ds(pl.multiple_of(base + spread * cols, 16), tile), :],
+                    source[pl.ds(pl.multiple_of(base + inner * (e * spread * cols), 16), tile), :]
+                    for e in plan[b]
                 ],
                 axis=1,
             )
             value = None
             for j in (0, -1, 1):
                 taps = jnp.concatenate(
-                    [dilated_w[9 * b + 3 * i + j + 1, :, lanes] for i in range(3)], axis=1
+                    [dilated_w[9 * b + 3 * (1 + inner * e) + j + 1, :, lanes] for e in plan[b]],
+                    axis=1,
                 )
                 piece = dot_nt(window, taps)
                 if j != 0:
@@ -235,17 +251,24 @@
             results.append(value)
         return results
 
+    def cells_of(half):
+        return pl.ds(pl.multiple_of(half * tile, 16), tile)
+
+    def gather_sums(source, half, part, plan, with_point, fresh):
+        for b, value in enumerate(branch_sums(source, half, part, plan, with_point)):
+            if value is None:
+                continue
+            if fresh:
+                acc[b, cells_of(half), :] = value
+            else:
+                acc[b, cells_of(half), :] += value
+
+    every = (-1, 0, 1)
     own_halo.wait()
-
-    def own_tile(k, carry):
-        base = first + k * tile
-        for b, value in enumerate(branch_sums(own, base, 0)):
-            acc[b, pl.ds(pl.multiple_of(k * tile, 16), tile), :] = value
-        return carry
-
-    lax.fori_loop(0, tiles, own_tile, 0)
-
-    next_rim.wait_recv()
+    gather_sums(own, inner_half, 0, (every, every, every), True, True)
+    gather_sums(own, outer_half, 0, (every, every, (0, 1)), True, True)
+
+    next_early.wait_recv()
     next_halo.start()
 
     frame_total.wait()
@@ -262,14 +285,20 @@
     width = point_w.shape[0]
     bias = dot_nt(feature, proj_w[:, pl.ds(4 * width, width)])[0:1]
 
-    next_rim.wait_send()
+    def choose(start, count):
+        @pl.loop(0, count // 2)
+        def _(k):
+            spot = pl.ds(pl.multiple_of(start + k * 2 * cols, 16), 2 * cols)
+            nxt[spot, :] = jnp.where(clip_end, own[spot, :], nxt[spot, :])
+
+    next_early.wait_send()
+    next_halo.wait()
+    choose(early_mine, EARLY)
+    choose(pl.multiple_of((REACH + rows) * cols * (1 - r), 16), REACH)
+    gather_sums(nxt, inner_half, 1, ((0, 1), (0, 1), (0, 1)), True, False)
+    gather_sums(nxt, outer_half, 1, ((), (1,), (1,)), False, False)
     next_rest.wait()
-    next_halo.wait()
-
-    @pl.loop(0, (rows + 2 * REACH) // 4)
-    def _(k):
-        spot = pl.ds(pl.multiple_of(k * 4 * cols, 16), 4 * cols)
-        nxt[spot, :] = jnp.where(clip_end, own[spot, :], nxt[spot, :])
+    choose(rest_mine, rows - EARLY)
 
     edge_src = pl.multiple_of((HEAD_REACH + (rows - HEAD_REACH) * (1 - r)) * cols, 16)
     edge_dst = pl.multiple_of((HEAD_REACH + rows) * cols * r, 16)
@@ -280,30 +309,24 @@
         (g, t, sister),
     )
 
-    def next_tile(s, carry):
-        k = r * s + (1 - r) * (tiles - 1 - s)
-        base = first + k * tile
-        spot = pl.ds(pl.multiple_of(k * tile, 16), tile)
+    def project(half, plan, with_point):
         mixed = bias
-        for b, value in enumerate(branch_sums(nxt, base, 1)):
-            branch = jnp.maximum(value + acc[b, spot, :], 0.0).astype(jnp.bfloat16)
+        for b, value in enumerate(branch_sums(nxt, half, 1, plan, with_point)):
+            full = acc[b, cells_of(half), :]
+            if value is not None:
+                full = full + value
+            branch = jnp.maximum(full, 0.0).astype(jnp.bfloat16)
             mixed = mixed + dot_nt(branch, proj_w[:, pl.ds(b * width, width)])
-        projected[pl.ds(pl.multiple_of((HEAD_REACH * cols) + k * tile, 16), tile), :] = jnp.maximum(
-            mixed, 0.0
-        ).astype(jnp.bfloat16)
-
-        @pl.when(s == 0)
-        def _():
-            edge_copy.start()
-
-        return carry
-
-    lax.fori_loop(0, tiles, next_tile, 0)
-    edge_copy.wait()
+        spot = pl.ds(pl.multiple_of(HEAD_REACH * cols + half * tile, 16), tile)
+        projected[spot, :] = jnp.maximum(mixed, 0.0).astype(jnp.bfloat16)
+
+    project(inner_half, ((-1,), (-1,), (-1,)), False)
+    edge_copy.start()
+    project(outer_half, (every, (-1, 0), (0,)), True)
 
     size = 2 * HEAD_REACH + 1
 
-    def head_tile(k, carry):
+    def head_tile(k):
         base = HEAD_REACH * cols + k * tile
         window = jnp.concatenate(
             [
@@ -328,9 +351,10 @@
             pred_ref[0, c, pl.ds(pl.multiple_of(k * tile_rows, 8), tile_rows), :] = (
                 jnp.concatenate([value[c : c + 1] for value in maps], axis=0)
             )
-        return carry
-
-    lax.fori_loop(0, tiles, head_tile, 0)
+
+    head_tile(outer_half)
+    edge_copy.wait()
+    head_tile(inner_half)
 
     gap = pred_ref[0, 0] - heat_map[...]
     offset_gap = jnp.abs(pred_ref[0, 1] - aim_map[0]) + jnp.abs(pred_ref[0, 2] - aim_map[1])
@@ -340,30 +364,26 @@
         jnp.where(counted, offset_gap, 0.0), axis=0, keepdims=True
     )
     err[2:3, pl.ds(0, cols)] = jnp.sum(jnp.where(counted, 1.0, 0.0), axis=0, keepdims=True)
-    pair = remote(7, err, err_in, (g, t, sister))
-    pair.start()
-    pair.wait()
-    err_pair[...] = err[...] + err_in[...]
-    err_all[t] = err_pair[...]
+    err_all[mine] = err[...]
 
     def spread_copy(step, slot):
         return pltpu.make_async_remote_copy(
-            src_ref=err_pair,
+            src_ref=err,
             dst_ref=err_all.at[slot],
             send_sem=all_send_sem.at[step],
             recv_sem=all_recv_sem.at[slot],
-            device_id=(g, others[step], r),
+            device_id=(g, slots[step] // 2, slots[step] % 2),
             device_id_type=MESH,
         )
 
-    for step in range(frame_count - 1):
-        spread_copy(step, t).start()
-    for step in range(frame_count - 1):
-        spread_copy(step, t).wait_send()
-        spread_copy(step, others[step]).wait_recv()
+    for step in range(bands - 1):
+        spread_copy(step, mine).start()
+    for step in range(bands - 1):
+        spread_copy(step, mine).wait_send()
+        spread_copy(step, slots[step]).wait_recv()
     summed = err_all[0]
-    for frame in range(1, frame_count):
-        summed = summed + err_all[frame]
+    for slot in range(1, bands):
+        summed = summed + err_all[slot]
     sums = jnp.sum(summed, axis=1, keepdims=True)
     center_loss = sums[0:1] / (frame_count * 2 * cells)
     offset_loss = offset_weight * sums[1:2] / jnp.maximum(sums[2:3], 1.0)
@@ -387,7 +407,7 @@
     cells = rows * cols
     frame_count = clip_start.shape[0]
     width = aspp_point.shape[0]
-    tile_rows = 16
+    tile_rows = rows // 2
     place = np.zeros((8, cells), np.float32)
     place[0] = 1.0
     place[1] = np.arange(cells) // cols
@@ -437,14 +457,12 @@
             pltpu.VMEM((8, channels), f32),
             pltpu.VMEM((8, channels), f32),
             pltpu.VMEM((8, LANES), f32),
-            pltpu.VMEM((8, LANES), f32),
-            pltpu.VMEM((8, LANES), f32),
-            pltpu.VMEM((frame_count, 8, LANES), f32),
+            pltpu.VMEM((2 * frame_count, 8, LANES), f32),
             pltpu.SemaphoreType.DMA((6,)),
-            pltpu.SemaphoreType.DMA((8,)),
-            pltpu.SemaphoreType.DMA((8,)),
-            pltpu.SemaphoreType.DMA((frame_count - 1,)),
-            pltpu.SemaphoreType.DMA((frame_count,)),
+            pltpu.SemaphoreType.DMA((7,)),
+            pltpu.SemaphoreType.DMA((7,)),
+            pltpu.SemaphoreType.DMA((2 * frame_count - 1,)),
+            pltpu.SemaphoreType.DMA((2 * frame_count,)),
         ],
         compiler_params=pltpu.CompilerParams(
             collective_id=0, has_side_effects=True, vmem_limit_bytes=56 * 1024 * 1024

time: 49.8 us -> 50.7 us (1.018)
  Pallas kernels: 46.4 us -> 47.3 us
    pallas_call x1, Pallas kernels: 46.4 us -> 47.3 us  [shards(): pl.pallas_call(functools.partial(kernel, frame_count, rows, cols, tile_ro...]
where the time goes in v4:
time: 50.7 us; the launch traced here: 50.5 us
  Pallas kernels  47.3 us (93%)
  local copies, waits for them, and re-layouts  2.59 us (5%)
  between operations  0.64 us (1%)
    pallas_call x1, Pallas kernels, shards(): pl.pallas_call(functools.partial(kernel, frame_count, rows, cols, tile_ro...  47.3 us
    unnamed x2, local copies, waits for them, and re-layouts  2.59 us

profile of v4, /device:TPU:0, one launch (start us, length us, event | category | flops | bytes accessed | tf_op | source)
XLA Modules:
  0.0 50.5 jit_solution(1923164932305015538)
XLA Ops:
  0.6 47.3 %shard_map.122 = (f32[1,4,32,48]{3,2,1,0:T(8,128)}, f32[2]{0:T(128)}) custom-call(bf16[1536,256]{1,0:T(8,128)(2,1)} %bitcast.5, s32[8]{0:T(128)} %clip_ref.1, s32[1,32,48]{2,1,0:T(8,128)} %semantic_ref.1, s32[1,32,48]{2,1,0:T(8,128)} %instance_ref.1, f32[8,1536]{1,0:T(8,128)} %constant.2.clone.place_ref, bf16[256,512]{1,0:T(8,128)(2,1)} %point_hbm.1, ...), custom_call_target="tpu_custom_call" | custom-call | tf_op jit(solution)/shard_map/pallas_call | solution.py:422
  47.9 1.5 %copy.15 = f32[1,4,32,48]{3,2,1,0:T(8,128)} copy(f32[1,4,32,48]{3,2,1,0:T(8,128)} %get-tuple-element.4) | data formatting | bytes 49152
  49.4 1.1 %copy.16 = f32[2]{0:T(128)} copy(f32[2]{0:T(128)} %get-tuple-element.5) | data formatting | bytes 16

commit v5 on v4

--- a/solution.py
+++ b/solution.py
@@ -202,19 +202,23 @@
     for copy in copies[1:]:
         copy.wait()
 
-    col = lax.broadcasted_iota(jnp.int32, (tile_rows, cols, LANES), 1).reshape(tile, LANES)
-
-    def widened(mask, width):
-        return jnp.concatenate([mask] * (width // LANES), axis=1)
+    def useful(step):
+        low = max(step, 0) // 16 * 16
+        high = -((-(cols + min(step, 0))) // 16) * 16
+        return low, high
 
     def moved(value, step):
+        if step == 0:
+            return value
+        low, high = useful(step)
         width = value.shape[1]
-        turned = pltpu.roll(value, (-step) % tile, 0)
+        lines = value.reshape(tile_rows, high - low, width)
+        blank = jnp.zeros((tile_rows, abs(step), width), value.dtype)
         if step > 0:
-            keep = col < cols - step
+            joined = [lines[:, step - low : cols - low], blank]
         else:
-            keep = col >= -step
-        return jnp.where(widened(keep, width), turned, 0.0)
+            joined = [blank, lines[:, : cols + step]]
+        return jnp.concatenate(joined, axis=1).reshape(tile, width)
 
     inner = 1 - 2 * r
     outer_half = r * (tiles - 1)
@@ -223,13 +227,12 @@
     def branch_sums(source, half, part, plan, with_point):
         lanes = pl.ds(part * channels, channels)
         base = first + half * tile
-        results = [None]
+        results = [None] * 10
         if with_point:
             rows_here = source[pl.ds(pl.multiple_of(base, 16), tile), :]
-            results = [dot_nt(rows_here, point_w[:, lanes])]
+            results[0] = dot_nt(rows_here, point_w[:, lanes])
         for b, spread in enumerate(DILATIONS):
             if not plan[b]:
-                results.append(None)
                 continue
             window = jnp.concatenate(
                 [
@@ -238,30 +241,30 @@
                 ],
                 axis=1,
             )
-            value = None
-            for j in (0, -1, 1):
+            lines = window.reshape(tile_rows, cols, window.shape[1])
+            for j in (-1, 0, 1):
                 taps = jnp.concatenate(
                     [dilated_w[9 * b + 3 * (1 + inner * e) + j + 1, :, lanes] for e in plan[b]],
                     axis=1,
                 )
-                piece = dot_nt(window, taps)
-                if j != 0:
-                    piece = moved(piece, j * spread)
-                value = piece if value is None else value + piece
-            results.append(value)
+                low, high = useful(j * spread)
+                part_lines = lines[:, low:high].reshape(-1, window.shape[1])
+                results[3 * b + j + 2] = dot_nt(part_lines, taps)
         return results
 
-    def cells_of(half):
-        return pl.ds(pl.multiple_of(half * tile, 16), tile)
+    def spot_of(slot, half):
+        lateral = (slot - 1) % 3 - 1 if slot else 0
+        low, high = useful(lateral * DILATIONS[(slot - 1) // 3] if slot else 0)
+        return pl.ds(pl.multiple_of(half * tile, 16), tile_rows * (high - low))
 
     def gather_sums(source, half, part, plan, with_point, fresh):
-        for b, value in enumerate(branch_sums(source, half, part, plan, with_point)):
+        for slot, value in enumerate(branch_sums(source, half, part, plan, with_point)):
             if value is None:
                 continue
             if fresh:
-                acc[b, cells_of(half), :] = value
+                acc[slot, spot_of(slot, half), :] = value
             else:
-                acc[b, cells_of(half), :] += value
+                acc[slot, spot_of(slot, half), :] += value
 
     every = (-1, 0, 1)
     own_halo.wait()
@@ -310,11 +313,21 @@
     )
 
     def project(half, plan, with_point):
+        sums = []
+        for slot, value in enumerate(branch_sums(nxt, half, 1, plan, with_point)):
+            full = acc[slot, spot_of(slot, half), :]
+            sums.append(full if value is None else full + value)
         mixed = bias
-        for b, value in enumerate(branch_sums(nxt, half, 1, plan, with_point)):
-            full = acc[b, cells_of(half), :]
-            if value is not None:
-                full = full + value
+        for b in range(4):
+            if b == 0:
+                full = sums[0]
+            else:
+                spread = DILATIONS[b - 1]
+                full = (
+                    sums[3 * b - 1]
+                    + moved(sums[3 * b - 2], -spread)
+                    + moved(sums[3 * b], spread)
+                )
             branch = jnp.maximum(full, 0.0).astype(jnp.bfloat16)
             mixed = mixed + dot_nt(branch, proj_w[:, pl.ds(b * width, width)])
         spot = pl.ds(pl.multiple_of(HEAD_REACH * cols + half * tile, 16), tile)
@@ -442,7 +455,7 @@
         scratch_shapes=[
             pltpu.VMEM((tall, channels), bf16),
             pltpu.VMEM((tall, channels), bf16),
-            pltpu.VMEM((4, cells, width), f32),
+            pltpu.VMEM((10, cells, width), f32),
             pltpu.VMEM(aspp_point.shape, bf16),
             pltpu.VMEM((taps,) + aspp_dilated.shape[2:], bf16),
             pltpu.VMEM(pool_weight.shape, bf16),

time: 50.7 us -> 50 us (0.986)
  Pallas kernels: 47.3 us -> 46.6 us
    pallas_call x1, Pallas kernels: 47.3 us -> 46.6 us  [shards(): pl.pallas_call(functools.partial(kernel, frame_count, rows, cols, tile_ro...]
where the time goes in v5:
time: 50 us; the launch traced here: 49.8 us
  Pallas kernels  46.6 us (93%)
  local copies, waits for them, and re-layouts  2.59 us (5%)
  between operations  0.64 us (1%)
    pallas_call x1, Pallas kernels, shards(): pl.pallas_call(functools.partial(kernel, frame_count, rows, cols, tile_ro...  46.6 us
    unnamed x2, local copies, waits for them, and re-layouts  2.59 us

profile of v5, /device:TPU:0, one launch (start us, length us, event | category | flops | bytes accessed | tf_op | source)
XLA Modules:
  0.0 49.8 jit_solution(12784340001326496957)
XLA Ops:
  0.6 46.6 %shard_map.122 = (f32[1,4,32,48]{3,2,1,0:T(8,128)}, f32[2]{0:T(128)}) custom-call(bf16[1536,256]{1,0:T(8,128)(2,1)} %bitcast.5, s32[8]{0:T(128)} %clip_ref.1, s32[1,32,48]{2,1,0:T(8,128)} %semantic_ref.1, s32[1,32,48]{2,1,0:T(8,128)} %instance_ref.1, f32[8,1536]{1,0:T(8,128)} %constant.2.clone.place_ref, bf16[256,512]{1,0:T(8,128)(2,1)} %point_hbm.1, ...), custom_call_target="tpu_custom_call" | custom-call | tf_op jit(solution)/shard_map/pallas_call | solution.py:435
  47.2 1.5 %copy.15 = f32[1,4,32,48]{3,2,1,0:T(8,128)} copy(f32[1,4,32,48]{3,2,1,0:T(8,128)} %get-tuple-element.4) | data formatting | bytes 49152
  48.7 1.1 %copy.16 = f32[2]{0:T(128)} copy(f32[2]{0:T(128)} %get-tuple-element.5) | data formatting | bytes 16

commit v6 on v5

--- a/solution.py
+++ b/solution.py
@@ -141,7 +141,6 @@
     )
     own_halo.start()
     next_early.start()
-    next_rest.start()
 
     own[pl.ds(halo_zero, rim), :] = jnp.zeros((rim, channels), own.dtype)
     nxt[pl.ds(halo_zero, rim), :] = jnp.zeros((rim, channels), nxt.dtype)
@@ -269,6 +268,8 @@
     every = (-1, 0, 1)
     own_halo.wait()
     gather_sums(own, inner_half, 0, (every, every, every), True, True)
+    next_early.wait_send()
+    next_rest.start()
     gather_sums(own, outer_half, 0, (every, every, (0, 1)), True, True)
 
     next_early.wait_recv()
@@ -294,7 +295,6 @@
             spot = pl.ds(pl.multiple_of(start + k * 2 * cols, 16), 2 * cols)
             nxt[spot, :] = jnp.where(clip_end, own[spot, :], nxt[spot, :])
 
-    next_early.wait_send()
     next_halo.wait()
     choose(early_mine, EARLY)
     choose(pl.multiple_of((REACH + rows) * cols * (1 - r), 16), REACH)

time: 50 us -> 47 us (0.940)
  Pallas kernels: 46.6 us -> 43.5 us
    pallas_call x1, Pallas kernels: 46.6 us -> 43.5 us  [shards(): pl.pallas_call(functools.partial(kernel, frame_count, rows, cols, tile_ro...]
where the time goes in v6:
time: 47 us; the launch traced here: 46.8 us
  Pallas kernels  43.5 us (93%)
  local copies, waits for them, and re-layouts  2.59 us (6%)
  between operations  0.64 us (1%)
    pallas_call x1, Pallas kernels, shards(): pl.pallas_call(functools.partial(kernel, frame_count, rows, cols, tile_ro...  43.5 us
    unnamed x2, local copies, waits for them, and re-layouts  2.59 us

profile of v6, /device:TPU:0, one launch (start us, length us, event | category | flops | bytes accessed | tf_op | source)
XLA Modules:
  0.0 46.8 jit_solution(472888383472170275)
XLA Ops:
  0.6 43.5 %shard_map.122 = (f32[1,4,32,48]{3,2,1,0:T(8,128)}, f32[2]{0:T(128)}) custom-call(bf16[1536,256]{1,0:T(8,128)(2,1)} %bitcast.5, s32[8]{0:T(128)} %clip_ref.1, s32[1,32,48]{2,1,0:T(8,128)} %semantic_ref.1, s32[1,32,48]{2,1,0:T(8,128)} %instance_ref.1, f32[8,1536]{1,0:T(8,128)} %constant.2.clone.place_ref, bf16[256,512]{1,0:T(8,128)(2,1)} %point_hbm.1, ...), custom_call_target="tpu_custom_call" | custom-call | tf_op jit(solution)/shard_map/pallas_call | solution.py:435
  44.2 1.5 %copy.15 = f32[1,4,32,48]{3,2,1,0:T(8,128)} copy(f32[1,4,32,48]{3,2,1,0:T(8,128)} %get-tuple-element.4) | data formatting | bytes 49152
  45.6 1.1 %copy.16 = f32[2]{0:T(128)} copy(f32[2]{0:T(128)} %get-tuple-element.5) | data formatting | bytes 16
